TPU v7x, 512 devices: a whole 4x8x8 slice. The times are simulated.
512 devices in a mesh: head: 8 (over x, core), inner: 4 (over y_lo), outer: 16 (over y_hi, z).
Axes of the slice: x: 4, y: 8 (y_hi: 2, y_lo: 4; y = y_hi * 4 + y_lo), z: 8, core: 2. Of those that a mesh axis runs over, the one named last changes fastest.
Arguments:
- query: bfloat16 [8192, 4096], P(('outer', 'inner', 'head')), may hold values from -80 to 80
- key: bfloat16 [8192, 1024], P(('outer', 'inner', 'head')), may hold values from -6 to 6
- value: bfloat16 [8192, 1024], P(('outer', 'inner', 'head')), may hold values from -6 to 6
- doc_lengths: int32 [24], replicated, may hold values from 1 to 2048, 8192 in all
- resid: bfloat16 [8192, 4096], P('outer', 'inner'), may hold values from -20 to 20
- norm_gain: float32 [4096], P('inner'), may hold values from 0.1 to 1.9
- w_out: bfloat16 [4096, 4096], P('head', ('inner', 'outer')), may hold values from -0.09375 to 0.09375
- w_gate_up: bfloat16 [2, 4096, 7168], P(None, ('inner', 'outer'), 'head'), may hold values from -0.09375 to 0.09375
- w_down: bfloat16 [7168, 4096], P('head', ('inner', 'outer')), may hold values from -0.0625 to 0.0625
Outputs:
- context: bfloat16 [8192, 4096], P(('outer', 'inner'), 'head')
- layer_out: bfloat16 [8192, 4096], P(('outer', 'head'), 'inner')
Inputs may be any that keep to these rules, and one draw needn't show every extreme that they name: `doc_lengths`: the 24 lengths sum to 8192, and the longest is exactly 2048.
All inputs are finite; a program needn't handle non-finite values.
Results may differ from a plain program's by a relative error of at most 0.03.
Values may be sent and summed in bfloat16 or wider, within the bound.
A program may use at most 64 MiB of HBM per device.

v0:
```python
import jax
import jax.numpy as jnp
from jax import lax
from jax.sharding import PartitionSpec as P

D = 4096
QUERY_HEADS = 32
KEY_VALUE_HEADS = 8
HEAD_WIDTH = 128


def segment_ids(positions, bounds):
    return jnp.sum((bounds[None, :] <= positions[:, None]).astype(jnp.int32), axis=1)


def per_device(query, key, value, doc_lengths, resid, norm_gain, w_out, w_gate_up, w_down):
    inner_count = lax.axis_size("inner")
    outer_count = lax.axis_size("outer")
    head_count = lax.axis_size("head")
    cycle_block = lax.axis_index("outer") * inner_count + lax.axis_index("inner")
    weights_out, weights_gate_up, weights_down = (
        lax.all_gather(w_out, "outer", axis=1, tiled=True),
        lax.all_gather(w_gate_up, "outer", axis=1, tiled=True),
        lax.all_gather(w_down, "outer", axis=1, tiled=True),
    )
    local_query, local_key, local_value = (
        lax.all_to_all(query, "head", split_axis=1, concat_axis=0, tiled=True),
        lax.all_to_all(key, "head", split_axis=1, concat_axis=0, tiled=True),
        lax.all_to_all(value, "head", split_axis=1, concat_axis=0, tiled=True),
    )
    bounds = jnp.cumsum(doc_lengths)
    seq_rows = local_query.shape[0]
    kv_heads = local_key.shape[1] // HEAD_WIDTH
    group_width = QUERY_HEADS // KEY_VALUE_HEADS
    score_scale = HEAD_WIDTH ** (-0.5)
    query_place = cycle_block * seq_rows + jnp.arange(seq_rows, dtype=jnp.int32)
    query_segment = segment_ids(query_place, bounds)
    grouped_query = local_query.reshape(seq_rows, kv_heads, group_width, HEAD_WIDTH)
    portion = (
        lax.all_gather(local_key, ("inner", "outer"), axis=0, tiled=True),
        lax.all_gather(local_value, ("inner", "outer"), axis=0, tiled=True),
    )
    span_rows = portion[0].shape[0]
    gathered_row = jnp.arange(span_rows, dtype=jnp.int32)
    source = gathered_row // seq_rows
    key_place = (
        source % outer_count * inner_count + source // outer_count
    ) * seq_rows + gathered_row % seq_rows
    tile_keys = portion[0]
    tile_values = portion[1]
    count_keys = tile_keys.shape[0]
    key_segment = segment_ids(key_place, bounds)
    allowed = (
        (key_place[None, :] <= query_place[:, None])
        & (key_place[None, :] >= 0)
        & (key_segment[None, :] == query_segment[:, None])
    )
    running_max = jnp.full((kv_heads, group_width, seq_rows), -1e30, jnp.float32)
    scores = (
        jnp.einsum(
            "qkgd,nkd->kgqn",
            grouped_query,
            tile_keys.reshape(count_keys, kv_heads, HEAD_WIDTH),
            preferred_element_type=jnp.float32,
        )
        * score_scale
    )
    masked = jnp.where(allowed, scores, -1e30)
    new_max = jnp.maximum(running_max, jnp.max(masked, axis=-1))
    exp_scores = jnp.where(allowed, jnp.exp(masked - new_max[..., None]), 0.0)
    new_totals = jnp.sum(exp_scores, axis=-1)
    weighted = jnp.einsum(
        "kgqn,nkd->kgqd",
        exp_scores.astype(jnp.bfloat16),
        tile_values.reshape(count_keys, kv_heads, HEAD_WIDTH),
        preferred_element_type=jnp.float32,
    )
    final_state = (new_max, new_totals, weighted)
    running_max, totals, accumulated = final_state
    context = (
        jnp.transpose(accumulated / totals[..., None], (2, 0, 1, 3))
        .reshape(seq_rows, kv_heads * group_width * HEAD_WIDTH)
        .astype(jnp.bfloat16)
    )
    partial_proj = jnp.dot(
        lax.all_gather(context, "inner", axis=0, tiled=True),
        weights_out,
        preferred_element_type=jnp.float32,
    )
    projected = lax.psum(partial_proj.astype(jnp.bfloat16), "head").astype(jnp.float32)
    hidden_state = (resid.astype(jnp.float32) + projected).astype(jnp.bfloat16)
    state_wide = lax.optimization_barrier(hidden_state).astype(jnp.float32)
    square_sums = lax.psum(jnp.sum(state_wide * state_wide, axis=1), "inner")
    inverse = lax.rsqrt(square_sums / D + 1e-05)
    normed = (state_wide * inverse[:, None] * norm_gain[None, :]).astype(jnp.bfloat16)
    gate_up = jnp.einsum("td,kdf->ktf", normed, weights_gate_up, preferred_element_type=jnp.float32)
    gate_up = lax.psum(gate_up.astype(jnp.bfloat16), "inner").astype(jnp.float32)
    activated = (jax.nn.silu(gate_up[0]) * gate_up[1]).astype(jnp.bfloat16)
    share_rows = activated.shape[0] // head_count
    down_part = lax.psum_scatter(
        jnp.dot(activated, weights_down, preferred_element_type=jnp.float32).astype(jnp.bfloat16),
        "head",
        scatter_dimension=0,
        tiled=True,
    ).astype(jnp.float32)
    own_rows_state = lax.dynamic_slice_in_dim(
        state_wide, lax.axis_index("head") * share_rows, share_rows, 0
    )
    layer_out = (own_rows_state + down_part).astype(jnp.bfloat16)
    return (context, layer_out)


def solution(mesh):
    placed = (
        P(("outer", "inner", "head"), None),
        P(("outer", "inner", "head"), None),
        P(("outer", "inner", "head"), None),
        P(),
        P("outer", "inner"),
        P("inner"),
        P("head", ("inner", "outer")),
        P(None, ("inner", "outer"), "head"),
        P("head", ("inner", "outer")),
    )
    return jax.shard_map(
        per_device,
        mesh=mesh,
        in_specs=placed,
        out_specs=(P(("outer", "inner"), "head"), P(("outer", "head"), "inner")),
        check_vma=False,
    )
```

profile of v0, /device:TPU:1, one launch (start us, length us, event | category | flops | bytes accessed | tf_op | source)
XLA Modules:
  0.0 1182.4 jit_solution(9292547899588832357)
XLA Ops:
  7.9 14.6 %all_to_all.54 = bf16[16,8,128]{2,0,1:T(8,128)(2,1)} all-to-all(bf16[16,8,128]{2,0,1:T(8,128)(2,1)S(1)} %copy_bitcast_fusion.1), channel_id=1, replica_groups=mesh['head'=8,'inner'=4,'outer'=16] {'head'}, dimensions={1} | all-to-all | bytes 65536 | tf_op jit(solution)/shard_map/all_to_all | solution.py:28
  23.4 7.8 all_to_all.55
  33.5 4.0 all-to-all-start.1
  39.6 3.8 compare_and_fusion
  43.5 271.2 %all-gather.6.cloned.1.call-done = bf16[8192,128]{1,0:T(8,128)(2,1)} async-done(((bf16[128,128]{1,0:T(8,128)(2,1)}), bf16[8192,128]{1,0:T(8,128)(2,1)}) %all-gather.6.cloned.1.call-update) | async-done | bytes 2097168 | tf_op jit(solution)/shard_map/all_gather | solution.py:40
  314.7 3.8 fusion
  318.5 5.7 copy-done.1
  324.2 4.2 fusion.1
  328.3 279.8 %all-gather.8.cloned.1.call-done = bf16[8192,128]{0,1:T(8,128)(2,1)} async-done(((bf16[128,128]{0,1:T(8,128)(2,1)}), bf16[8192,128]{0,1:T(8,128)(2,1)}) %all-gather.8.cloned.1.call-update) | async-done | bytes 2097168 | tf_op jit(solution)/shard_map/all_gather | solution.py:41
  608.2 10.0 fusion.17
  618.2 12.4 %all_gather.20 = bf16[512,512]{0,1:T(8,128)(2,1)S(1)} all-gather(bf16[128,512]{0,1:T(8,128)(2,1)S(1)} %bitcast.86), channel_id=1, replica_groups=mesh['head'=8,'inner'=4,'outer'=16] {'inner'}, dimensions={0}, use_global_device_ids=true | all-gather | bytes 655360 | tf_op jit(solution)/shard_map/all_gather | solution.py:86
  630.7 104.1 %all-gather.10.cloned.1.call-done = bf16[512,1024]{0,1:T(8,128)(2,1)} async-done(((bf16[512,64]{0,1:T(8,128)(2,1)}), bf16[512,1024]{0,1:T(8,128)(2,1)}) %all-gather.10.cloned.1.call-update) | async-done | bytes 1048592 | tf_op jit(solution)/shard_map/all_gather | solution.py:22
  734.8 2.9 convolution_convert_fusion.1
  738.4 71.7 %all-reduce.3.cloned.1.call-done = bf16[512,1024]{1,0:T(8,128)(2,1)} async-done(((bf16[512,1024]{1,0:T(8,128)(2,1)}), bf16[512,1024]{1,0:T(8,128)(2,1)}) %all-reduce.3.cloned.1.call-update) | async-done | bytes 1048592 | tf_op jit(solution)/shard_map/psum | solution.py:90
  810.1 1.6 add_convert_fusion
  812.0 9.2 psum.22
  821.2 113.7 %all-gather.12.cloned.1.call-done = bf16[2,1024,896]{2,1,0:T(8,128)(2,1)} async-done(((bf16[2,64,896]{2,1,0:T(8,128)(2,1)}), bf16[2,1024,896]{2,1,0:T(8,128)(2,1)}) %all-gather.12.cloned.1.call-update) | async-done | bytes 3670032 | tf_op jit(solution)/shard_map/all_gather | solution.py:23
  935.0 5.5 convert_bitcast_fusion
  941.3 92.8 %all-reduce.5.cloned.1.call-done = bf16[2,512,896]{2,1,0:T(8,128)(2,1)} async-done(((bf16[2,512,896]{2,1,0:T(8,128)(2,1)}), bf16[2,512,896]{2,1,0:T(8,128)(2,1)}) %all-reduce.5.cloned.1.call-update) | async-done | bytes 1835024 | tf_op jit(solution)/shard_map/psum | solution.py:97
  1034.1 3.5 convert_element_type.75
  1037.6 95.4 %all-gather.14.cloned.1.call-done = bf16[896,1024]{0,1:T(8,128)(2,1)} async-done(((bf16[896,64]{0,1:T(8,128)(2,1)}), bf16[896,1024]{0,1:T(8,128)(2,1)}) %all-gather.14.cloned.1.call-update) | async-done | bytes 1835024 | tf_op jit(solution)/shard_map/all_gather | solution.py:24
  1133.1 4.9 convolution_convert_fusion
  1139.0 35.0 %reduce-scatter.2.cloned.1.call-done = bf16[64,1024]{1,0:T(8,128)(2,1)} async-done(((bf16[512,1024]{1,0:T(8,128)(2,1)}), bf16[64,1024]{1,0:T(8,128)(2,1)}) %reduce-scatter.2.cloned.1.call-update) | async-done | bytes 131088 | tf_op jit(solution)/shard_map/reduce_scatter | solution.py:100
  1174.0 1.6 add_convert_fusion.1
  (42 shorter events, 8.7 us)
Async XLA Ops:
  7.2 0.8 copy-start
  7.2 307.5 %all-gather.6.cloned.1.call-start = ((), (), s32[]{:S(2)}) async-start(), calls=%async_computation.4 | async-start | bytes 2129920 | tf_op jit(solution)/shard_map/all_gather | solution.py:40
  22.6 585.6 %all-gather.8.cloned.1.call-start = ((), (), s32[]{:S(2)}) async-start(), calls=%async_computation.5 | async-start | bytes 2129920 | tf_op jit(solution)/shard_map/all_gather | solution.py:41
  33.5 9.9 all-to-all-start.1
  37.5 697.2 %all-gather.10.cloned.1.call-start = ((), (), s32[]{:S(2)}) async-start(), calls=%async_computation.6 | async-start | bytes 1114112 | tf_op jit(solution)/shard_map/all_gather | solution.py:22
  38.3 771.8 %all-reduce.3.cloned.1.call-start = ((), (), s32[]{:S(2)}) async-start(), calls=%async_computation.7 | async-start | bytes 2097152 | tf_op jit(solution)/shard_map/psum | solution.py:90
  318.5 5.7 copy-start.1
  618.2 191.9 %copy-start.2 = (bf16[512,1024]{1,0:T(8,128)(2,1)S(1)}, bf16[512,1024]{1,0:T(8,128)(2,1)}, u32[]{:S(2)}) copy-start(bf16[512,1024]{1,0:T(8,128)(2,1)} %param.13) | copy-start | bytes 3145732
  630.7 304.3 %copy-start.3 = (f32[1024]{0:T(1024)S(1)}, f32[1024]{0:T(1024)}, u32[]{:S(2)}) copy-start(f32[1024]{0:T(1024)} %param.14) | copy-start | bytes 12292
  737.7 197.2 %all-gather.12.cloned.1.call-start = ((), (), s32[]{:S(2)}) async-start(), calls=%async_computation.8 | async-start | bytes 3899392 | tf_op jit(solution)/shard_map/all_gather | solution.py:23
  738.3 295.8 %all-reduce.5.cloned.1.call-start = ((), (), s32[]{:S(2)}) async-start(), calls=%async_computation.9 | async-start | bytes 3670016 | tf_op jit(solution)/shard_map/psum | solution.py:97
  940.5 192.6 %all-gather.14.cloned.1.call-start = ((), (), s32[]{:S(2)}) async-start(), calls=%async_computation.10 | async-start | bytes 1949696 | tf_op jit(solution)/shard_map/all_gather | solution.py:24
  941.2 232.7 %reduce-scatter.2.cloned.1.call-start = ((), (), s32[]{:S(2)}) async-start(), calls=%async_computation.11 | async-start | bytes 1179648 | tf_op jit(solution)/shard_map/reduce_scatter | solution.py:100
Sparse Core Ops, SparseCore 0:
  22.7 291.9 all-gather.5
  317.3 290.8 all-gather.7
  611.3 123.3 all-gather.9
  737.9 72.1 all-reduce.2
  813.1 121.7 all-gather.11
  940.6 93.4 all-reduce.4
  1037.3 95.7 all-gather.13
  1138.1 35.8 reduce-scatter.1
where the time goes:
time: 1180 us
  waiting for transfers between devices  1070 us (91%)
  blocking collectives  44.1 us (4%)
  matrix products  27.1 us (2%)
  other arithmetic  15.8 us (1%)
  between operations  14.3 us (1%)
    all_gather x1, waiting for transfers between devices, per_device(): lax.all_gather(local_value, ('inner', 'outer'), axis=0, tiled=True)  280 us
    all_gather x1, waiting for transfers between devices, per_device(): lax.all_gather(local_key, ('inner', 'outer'), axis=0, tiled=True)  271 us
    all_gather x1, waiting for transfers between devices, per_device(): lax.all_gather(w_gate_up, 'outer', axis=1, tiled=True)  114 us
    all_gather x1, waiting for transfers between devices, per_device(): lax.all_gather(w_out, 'outer', axis=1, tiled=True)  104 us
    all_gather x1, waiting for transfers between devices, per_device(): lax.all_gather(w_down, 'outer', axis=1, tiled=True)  95.4 us
    psum x1, waiting for transfers between devices, per_device(): lax.psum(gate_up.astype(jnp.bfloat16), 'inner').astype(jnp.float32)  92.8 us
    psum x1, waiting for transfers between devices, per_device(): lax.psum(partial_proj.astype(jnp.bfloat16), 'head').astype(jnp.float32)  71.7 us
    reduce_scatter x1, waiting for transfers between devices, per_device(): lax.psum_scatter(jnp.dot(activated, weights_down, preferred_element_type=...  35 us
  transfers between devices with their start and end apart: 9, of which 8 were waited for; matrix products, arithmetic and copies ran while one was open for 3% of the time, Pallas kernels for 0%

commit v1 on v0

v1 whole, which is shorter than its diff:
```python
import jax
import jax.numpy as jnp
from jax import lax
from jax.experimental import pallas as pl
from jax.experimental.pallas import tpu as pltpu
from jax.sharding import PartitionSpec as P

MESH = pl.DeviceIdType.MESH
D = 4096
BF = jnp.bfloat16
F32 = jnp.float32
SCALE = 128 ** (-0.5)
DOCS = 24
NX, NY, NZ = 4, 8, 8
BACK = 5


def nt(a, b):
    return lax.dot_general(a, b, (((1,), (1,)), ((), ())), preferred_element_type=F32)


def kernel(
    q_ref, k_ref, v_ref, docs_ref, resid_ref, gain_ref, wo_ref, wgu_ref, wd_ref,
    ctx_ref, out_ref,
    q_all, kv, scores, ctx_all, wo_all, w_all, res, gains,
    proj, proj_in, hid, acc, act, down, x_in, x_sum, y_in, ring_r, ring_l, odd_sum, odd_in,
    send_sem, recv_sem, local_sem,
):
    head = lax.axis_index("head")
    y_lo = lax.axis_index("inner")
    outer = lax.axis_index("outer")
    x, c = head // 2, head % 2
    y_hi, z = outer // NZ, outer % NZ
    y = y_hi * 4 + y_lo
    other = 1 - c

    def to_head(h):
        return {"head": h}

    def to_x(i):
        return {"head": i * 2 + c}

    def to_y(i):
        return {"inner": i % 4, "outer": (i // 4) * NZ + z}

    def to_z(i):
        return {"outer": y_hi * NZ + i}

    sibling = to_head(x * 2 + other)

    def feat(i):
        return (i % 4) * 2 + i // 4

    counter = [0]
    sends, locals_ = [], []

    def new(count=1):
        counter[0] += count
        return counter[0] - count

    def remote(src, dst, sid, dev):
        return pltpu.make_async_remote_copy(
            src_ref=src, dst_ref=dst, send_sem=send_sem.at[sid], recv_sem=recv_sem.at[sid],
            device_id=dev, device_id_type=MESH,
        )

    def push(src, dst, sid, dev):
        copy = remote(src, dst, sid, dev)
        copy.start()
        sends.append(copy)

    def arrive(dst, sid):
        remote(dst, dst, sid, sibling).wait_recv()

    local_count = [0]

    def local(src, dst):
        copy = pltpu.make_async_copy(src, dst, local_sem.at[local_count[0]])
        local_count[0] += 1
        copy.start()
        return copy

    def ring(n, me, to, chunk, half, arrived=None):
        steps = n // 2
        sr, sl = new(steps), new(steps)
        right, left = to((me + 1) % n), to((me + n - 1) % n)

        def run():
            for s in range(steps):
                back, ahead = (me - s + n) % n, (me + s) % n
                if s > 0:
                    arrive(chunk(back), sr + s - 1)
                    arrive(chunk(ahead), sl + s - 1)
                if s < steps - 1:
                    push(chunk(back), chunk(back), sr + s, right)
                    push(chunk(ahead), chunk(ahead), sl + s, left)
                else:
                    push(half(back, 0), half(back, 0), sr + s, right)
                    push(half(ahead, 1), half(ahead, 1), sl + s, left)
                if arrived is not None:
                    arrived(back, 2 * s)
                    if s > 0:
                        arrived(ahead, 2 * s - 1)
                yield
            far = (me + steps) % n
            arrive(half(far, 0), sr + steps - 1)
            arrive(half(far, 1), sl + steps - 1)
            if arrived is not None:
                arrived(far, 2 * steps - 1)

        return run()

    def finish(gen):
        for _ in gen:
            pass

    barrier = pltpu.get_barrier_semaphore()
    for k in range(1, 8):
        pl.semaphore_signal(barrier, inc=1, device_id=to_head((head + k) % 8), device_id_type=MESH)
        pl.semaphore_signal(barrier, inc=1, device_id=to_y((y + k) % NY), device_id_type=MESH)
        pl.semaphore_signal(barrier, inc=1, device_id=to_z((z + k) % NZ), device_id_type=MESH)
    pl.semaphore_wait(barrier, 21)

    kv_sid, q_sid = new(16), new(8)
    for k in range(1, 8):
        peer = (head + k) % 8
        cols = pl.ds(pl.multiple_of(peer * 128, 128), 128)
        push(k_ref.at[:, cols], kv.at[0, y, 0, head], kv_sid + k, to_head(peer))
        push(v_ref.at[:, cols], kv.at[0, y, 1, head], kv_sid + 8 + k, to_head(peer))
    own = pl.ds(pl.multiple_of(head * 128, 128), 128)
    kv[0, y, 0, head] = k_ref[:, own]
    kv[0, y, 1, head] = v_ref[:, own]
    for k in range(1, 8):
        peer = (head + k) % 8
        cols = pl.ds(pl.multiple_of(peer * 512, 512), 512)
        push(q_ref.at[:, cols], q_all.at[head], q_sid + k, to_head(peer))
    q_all[head] = q_ref[:, pl.ds(pl.multiple_of(head * 512, 512), 512)]

    for k in range(1, 8):
        peer = (head + 8 - k) % 8
        arrive(kv.at[0, y, 0, peer], kv_sid + k)
        arrive(kv.at[0, y, 1, peer], kv_sid + 8 + k)
    z_sid = new(BACK)
    for k in range(1, BACK):
        push(kv.at[0, y], kv.at[k, y], z_sid + k, to_z((z + k) % NZ))

    def lanes(core, width):
        return pl.ds(pl.multiple_of(core * width, width), width)

    def shared_ring(buf_chunk, buf_half):
        sid = new(8)
        gen = ring(
            NZ, z, to_z, lambda i: buf_chunk(i, c), lambda i, b: buf_half(i, b, c),
            lambda i, n: push(buf_chunk(i, c), buf_chunk(i, c), sid + n, sibling),
        )

        def wait_sibling():
            for n in range(8):
                step = (n + 1) // 2
                i = (z + step) % NZ if n % 2 else (z - step + NZ) % NZ
                arrive(buf_chunk(i, other), sid + n)

        return gen, wait_sibling

    wo_copy = local(wo_ref, wo_all.at[z, :, lanes(c, 512)])
    wo_ring, wo_wait = shared_ring(
        lambda i, s: wo_all.at[i, :, lanes(s, 512)],
        lambda i, b, s: wo_all.at[i, pl.ds(b * 32, 32), lanes(s, 512)],
    )

    res_rows = pl.ds(pl.multiple_of(head * 64, 64), 64)
    res_sid = new()
    push(
        resid_ref.at[res_rows, lanes(1 - y_hi, 512)], res.at[y_hi], res_sid,
        to_y((1 - y_hi) * 4 + y_lo),
    )
    res_copy = local(resid_ref.at[res_rows, lanes(y_hi, 512)], res.at[y_hi])
    gain_sid = new(4)
    for k in range(1, 4):
        push(gain_ref, gains.at[y_lo], gain_sid + k, to_y(y_hi * 4 + (y_lo + k) % 4))
    gains[y_lo] = gain_ref[...]

    kv_rings = [
        ring(
            NY, y, to_y,
            lambda i, dz=dz: kv.at[dz, i],
            lambda i, b, dz=dz: kv.at[dz, i, b],
        )
        for dz in range(BACK)
    ]
    for t in range(BACK + 4):
        for dz in range(BACK):
            if 0 <= t - dz <= 4:
                if t == dz and dz > 0:
                    arrive(kv.at[dz, y], z_sid + dz)
                next(kv_rings[dz], None)
        if t == 2:
            wo_copy.wait()
        if t >= 2:
            next(wo_ring, None)
    finish(wo_ring)

    w_sid = new(24)

    def w_cols(part, s):
        return pl.ds(pl.multiple_of(s * 384 + part * 128, 128), 128)

    def w_sources(i):
        cols = pl.ds(pl.multiple_of(i * 128, 128), 128)
        return wgu_ref.at[0, :, cols], wgu_ref.at[1, :, cols], wd_ref.at[:, cols]

    for k in range(1, NY):
        peer = (y + k) % NY

        @pl.when(peer != NY - 1)
        def _(k=k, peer=peer):
            for part, src in enumerate(w_sources(peer)):
                remote(
                    src, w_all.at[feat(y), z, :, w_cols(part, c)], w_sid + 3 * k + part, to_y(peer)
                ).start()

    @pl.when(y != NY - 1)
    def _():
        for part, src in enumerate(w_sources(y)):
            pltpu.make_async_copy(
                src, w_all.at[feat(y), z, :, w_cols(part, c)], local_sem.at[8 + part]
            ).start()

    @pl.when(y == NY - 1)
    def _():
        def zero(f, _):
            w_all[f, z, :, lanes(c, 384)] = jnp.zeros((64, 384), BF)
            return 0

        lax.fori_loop(0, 8, zero, 0)

    for k in range(1, 8):
        arrive(q_all.at[(head + 8 - k) % 8], q_sid + k)
    place = outer * 512 + y_lo * 128 + lax.broadcasted_iota(jnp.int32, (128, 1), 0)
    start = jnp.zeros((128, 1), jnp.int32)
    bound = jnp.int32(0)
    for j in range(DOCS):
        bound = bound + docs_ref[j]
        start = jnp.where(bound <= place, bound, start)
    for dz in range(BACK):
        half = jnp.where(z >= dz, y_hi, 1 - y_hi)
        keys = kv[dz, pl.ds(half * 4, 4), 0].reshape(512, 128)
        key_place = (outer - dz) * 512 + lax.broadcasted_iota(jnp.int32, (1, 512), 1)
        bias = jnp.where((key_place <= place) & (key_place >= start), 0.0, -1e30)
        for g in range(4):
            heads_q = q_all[:, :, g * 128:(g + 1) * 128].reshape(128, 128)
            scores[g, :, dz * 512:(dz + 1) * 512] = nt(heads_q, keys) * SCALE + bias
    for g in range(4):
        s = scores[g]
        e = jnp.exp(s - jnp.max(s, axis=1, keepdims=True))
        total = jnp.sum(e, axis=1, keepdims=True)
        e = e.astype(BF)
        summed = jnp.zeros((128, 128), F32)
        for dz in range(BACK):
            half = jnp.where(z >= dz, y_hi, 1 - y_hi)
            values = kv[dz, pl.ds(half * 4, 4), 1].reshape(512, 128)
            summed += jnp.dot(e[:, dz * 512:(dz + 1) * 512], values, preferred_element_type=F32)
        ctx_ref[:, g * 128:(g + 1) * 128] = (summed / total).astype(BF)

    def half_rows(i):
        return pl.ds(pl.multiple_of(i * 64, 64), 64)

    ctx_sid = new()
    push(ctx_ref.at[half_rows(other)], ctx_all.at[y, :, lanes(c, 512)], ctx_sid, sibling)
    ctx_all[y, :, lanes(c, 512)] = ctx_ref[half_rows(c), :]

    @pl.when(y != NY - 1)
    def _():
        for part, src in enumerate(w_sources(y)):
            pltpu.make_async_copy(
                src, w_all.at[feat(y), z, :, w_cols(part, c)], local_sem.at[8 + part]
            ).wait()
        for k in range(1, NY):
            for part in range(3):
                dst = w_all.at[feat((y + NY - k) % NY), z, :, w_cols(part, c)]
                arrive(dst, w_sid + 3 * k + part)

    w_ring, w_wait = shared_ring(
        lambda i, s: w_all.at[:, i, :, lanes(s, 384)],
        lambda i, b, s: w_all.at[pl.ds(b * 4, 4), i, :, lanes(s, 384)],
    )
    next(w_ring)
    arrive(ctx_all.at[y, :, lanes(other, 512)], ctx_sid)
    finish(ring(
        NY, y, to_y, lambda i: ctx_all.at[i], lambda i, b: ctx_all.at[i, pl.ds(b * 32, 32)]
    ))

    wo_wait()
    next(w_ring)

    def project(i, _):
        rows = ctx_all[pl.ds(i * 2, 2)].reshape(128, 1024)
        part = nt(rows, wo_all[...].reshape(512, 1024)).astype(BF).reshape(2, 64, 512)
        proj[i // 2, pl.ds((i % 2) * 2, 2)] = part
        return 0

    lax.fori_loop(0, 4, project, 0)
    proj_sid = new(4)
    for k in range(1, NX):
        peer = (x + k) % NX
        push(proj.at[:, peer], proj_in.at[k - 1], proj_sid + k, to_x(peer))
    res_copy.wait()
    arrive(res.at[1 - y_hi], res_sid)
    for k in range(1, NX):
        arrive(proj_in.at[k - 1], proj_sid + k)
    for g in range(2):
        total = proj[g, x].astype(F32)
        for k in range(3):
            total += proj_in[k, g].astype(F32)
        hid[feat(y), g, x] = (res[g].astype(F32) + total).astype(BF)

    first_sid, second_sid = new(4), new(32)

    def along_x(i, n):
        for k in range(1, NX):
            push(hid.at[feat(i), 1, x], hid.at[feat(i), 1, x], second_sid + 4 * n + k, to_x((x + k) % NX))

    for k in range(1, NX):
        push(hid.at[feat(y), 0, x], hid.at[feat(y), 0, x], first_sid + k, to_x((x + k) % NX))
    y_first = ring(
        NY, y, to_y, lambda i: hid.at[feat(i), 1, x],
        lambda i, b: hid.at[feat(i), 1, x, pl.ds(b * 32, 32)], along_x,
    )
    next(y_first)
    for k in range(1, NX):
        arrive(hid.at[feat(y), 0, (x + NX - k) % NX], first_sid + k)
    x_first = ring(
        NY, y, to_y, lambda i: hid.at[feat(i), 0],
        lambda i, b: hid.at[feat(i), 0, pl.ds(b * 2, 2)],
    )
    for s in range(4):
        next(x_first, None)
        next(y_first, None)
        if s in (0, 2):
            next(w_ring, None)
    finish(w_ring)
    finish(y_first)
    finish(x_first)
    for n in range(8):
        step = (n + 1) // 2
        i = (y + step) % NY if n % 2 else (y - step + NY) % NY
        for k in range(1, NX):
            arrive(hid.at[feat(i), 1, (x + NX - k) % NX], second_sid + 4 * n + k)
    for k in range(1, 4):
        arrive(gains.at[(y_lo + 4 - k) % 4], gain_sid + k)
    w_wait()

    acc[...] = jnp.zeros_like(acc)

    def gate_up(f, squares):
        parts = []
        gain_row = gains[f // 2]
        for m in range(2):
            rows = hid[f, m].reshape(256, 512).astype(F32)
            parts.append(jnp.sum(rows * rows, axis=1, keepdims=True))
            scaled = jnp.concatenate(
                [
                    rows[:, j * 128:(j + 1) * 128]
                    * jnp.where(f % 2 == 0, gain_row[j:j + 1], gain_row[4 + j:5 + j])
                    for j in range(4)
                ],
                axis=1,
            ).astype(BF)
            for s in range(2):
                weights = w_all[f, :, :, s * 384:s * 384 + 256].reshape(512, 256)
                acc[s, m * 256:(m + 1) * 256] += jnp.dot(scaled, weights, preferred_element_type=F32)
        return squares + jnp.concatenate(parts, axis=0)

    squares = lax.fori_loop(0, 8, gate_up, jnp.zeros((512, 1), F32))
    inverse = lax.rsqrt(squares / D + 1e-05)
    for s in range(2):
        gate, up = acc[s, :, :128] * inverse, acc[s, :, 128:] * inverse
        act[:, s * 128:(s + 1) * 128] = (gate / (1.0 + jnp.exp(-gate)) * up).astype(BF)

    def project_down(f, _):
        weights = jnp.concatenate(
            [w_all[f, :, :, s * 384 + 256:s * 384 + 384].reshape(512, 128) for s in range(2)], axis=1
        )
        for m in range(2):
            part = nt(act[m * 256:(m + 1) * 256], weights)
            down[f // 2, f % 2, m] = part.astype(BF).reshape(4, 64, 512)
        return 0

    lax.fori_loop(0, 8, project_down, 0)

    right_sid, left_sid, x_sid, y_sid, odd_sid = new(7), new(7), new(4), new(8), new(4)

    def odd(i, b):
        return down.at[i % 4, 1, i // 4, pl.ds(b * 2, 2)]

    to_right, to_left = to_y((y + 1) % NY), to_y((y + NY - 1) % NY)
    push(odd((y + NY - 1) % NY, 0), ring_r.at[0], right_sid, to_right)
    push(odd((y + 1) % NY, 1), ring_l.at[0], left_sid, to_left)
    for k in range(1, NX):
        peer = (x + k) % NX
        push(down.at[:, 0, :, peer], x_in.at[k - 1], x_sid + k, to_x(peer))

    def add_even():
        for k in range(1, NX):
            arrive(x_in.at[k - 1], x_sid + k)

        def add(i, _):
            total = down[i // 2, 0, i % 2, x].astype(F32)
            for k in range(3):
                total += x_in[k, i // 2, i % 2].astype(F32)
            x_sum[i // 2, i % 2] = total.astype(BF)
            return 0

        lax.fori_loop(0, 8, add, 0)
        for k in range(1, NY):
            peer = (y + k) % NY
            push(x_sum.at[peer % 4, peer // 4], y_in.at[k - 1], y_sid + k, to_y(peer))

    for s in range(7):
        if s == 5:
            add_even()
        back, ahead = (y + 2 * NY - 2 - s) % NY, (y + 2 + s) % NY
        for buf, sid, i, b, dev in (
            (ring_r, right_sid, back, 0, to_right), (ring_l, left_sid, ahead, 1, to_left)
        ):
            arrive(buf.at[s], sid + s)
            mine = down[i % 4, 1, i // 4, pl.ds(b * 2, 2)]
            total = (buf[s].astype(F32) + mine.astype(F32)).astype(BF)
            if s < 6:
                buf[s] = total
                push(buf.at[s], buf.at[s + 1], sid + s + 1, dev)
            else:
                odd_sum[b * 2:b * 2 + 2] = total
    for k in range(1, NX):
        peer = (x + k) % NX
        push(odd_sum.at[peer], odd_in.at[k - 1], odd_sid + k, to_x(peer))

    total = x_sum[y_lo, y_hi].astype(F32)
    for k in range(1, NY):
        arrive(y_in.at[k - 1], y_sid + k)
        total += y_in[k - 1].astype(F32)
    out_ref[:, :512] = (hid[2 * y_lo, y_hi, x].astype(F32) + total).astype(BF)
    total = odd_sum[x].astype(F32)
    for k in range(1, NX):
        arrive(odd_in.at[k - 1], odd_sid + k)
        total += odd_in[k - 1].astype(F32)
    out_ref[:, 512:] = (hid[2 * y_lo + 1, y_hi, x].astype(F32) + total).astype(BF)

    for copy in sends:
        copy.wait_send()
    for k in range(1, NY):
        peer = (y + k) % NY

        @pl.when(peer != NY - 1)
        def _(k=k, peer=peer):
            for part, src in enumerate(w_sources(peer)):
                remote(
                    src, w_all.at[feat(y), z, :, w_cols(part, c)], w_sid + 3 * k + part, to_y(peer)
                ).wait_send()

    assert counter[0] <= SEMS, counter[0]


SEMS = 256


def per_device(query, key, value, doc_lengths, resid, norm_gain, w_out, w_gate_up, w_down):
    vmem = pl.BlockSpec(memory_space=pltpu.VMEM)
    anywhere = pl.BlockSpec(memory_space=pl.ANY)
    smem = pl.BlockSpec(memory_space=pltpu.SMEM)

    def buf(*shape, kind=BF):
        return pltpu.VMEM(shape, kind)

    return pl.pallas_call(
        kernel,
        out_shape=(
            jax.ShapeDtypeStruct((128, 512), BF),
            jax.ShapeDtypeStruct((64, 1024), BF),
        ),
        in_specs=[vmem, vmem, vmem, smem, anywhere, vmem, anywhere, anywhere, anywhere],
        out_specs=(vmem, vmem),
        scratch_shapes=[
            buf(8, 16, 512),
            buf(BACK, 8, 2, 8, 16, 128),
            buf(4, 128, BACK * 512, kind=F32),
            buf(8, 64, 1024),
            buf(8, 64, 1024),
            buf(8, 8, 64, 768),
            buf(2, 64, 512),
            buf(4, 8, 128, kind=F32),
            buf(2, 4, 64, 512),
            buf(3, 2, 64, 512),
            buf(8, 2, 4, 64, 512),
            buf(2, 512, 256, kind=F32),
            buf(512, 256),
            buf(4, 2, 2, 4, 64, 512),
            buf(3, 4, 2, 64, 512),
            buf(4, 2, 64, 512),
            buf(7, 64, 512),
            buf(7, 2, 64, 512),
            buf(7, 2, 64, 512),
            buf(4, 64, 512),
            buf(3, 64, 512),
            pltpu.SemaphoreType.DMA((SEMS,)),
            pltpu.SemaphoreType.DMA((SEMS,)),
            pltpu.SemaphoreType.DMA((16,)),
        ],
        compiler_params=pltpu.CompilerParams(
            collective_id=0, has_side_effects=True, vmem_limit_bytes=56 * 1024 * 1024
        ),
        cost_estimate=pl.CostEstimate(flops=4_000_000_000, bytes_accessed=4_000_000, transcendentals=2_000_000),
    )(
        query, key, value, doc_lengths, resid, norm_gain.reshape(8, 128),
        w_out.T, w_gate_up, w_down.T,
    )


def solution(mesh):
    placed = (
        P(("outer", "inner", "head"), None),
        P(("outer", "inner", "head"), None),
        P(("outer", "inner", "head"), None),
        P(),
        P("outer", "inner"),
        P("inner"),
        P("head", ("inner", "outer")),
        P(None, ("inner", "outer"), "head"),
        P("head", ("inner", "outer")),
    )
    return jax.shard_map(
        per_device,
        mesh=mesh,
        in_specs=placed,
        out_specs=(P(("outer", "inner"), "head"), P(("outer", "head"), "inner")),
        check_vma=False,
    )
```

time: 1180 us -> 190 us (0.16)
  waiting for transfers between devices: 1070 us -> 0 us
  Pallas kernels: 0 us -> 184 us
  blocking collectives: 44.1 us -> 0 us
  matrix products: 27.1 us -> 0 us
  other arithmetic: 15.8 us -> 0 us
  between operations: 14.3 us -> 0.65 us
    all_gather x5 -> x0, waiting for transfers between devices: 864 us -> none  [the longest x1 280 us: per_device(): lax.all_gather(local_value, ('inner', 'outer'), axis=0, tiled=True)]
    pallas_call x0 -> x1, Pallas kernels: none -> 184 us  [per_device(): pl.pallas_call(kernel, out_shape=(jax.ShapeDtypeStruct((128, 512), BF), j...]
    psum x2 -> x0, waiting for transfers between devices: 165 us -> none  [the longest x1 92.8 us: per_device(): lax.psum(gate_up.astype(jnp.bfloat16), 'inner').astype(jnp.float32)]
    reduce_scatter x1 -> x0, waiting for transfers between devices: 35 us -> none  [per_device(): lax.psum_scatter(jnp.dot(activated, weights_down, preferred_element_type=...]
    dot_general x5 -> x0, matrix products: 27.1 us -> none  [the longest x1 10 us: per_device(): jnp.einsum('kgqn,nkd->kgqd', exp_scores.astype(jnp.bfloat16), tile_values...]
    all_to_all x2 -> x0, blocking collectives: 22.4 us -> none  [the longest x1 14.6 us: per_device(): lax.all_to_all(key, 'head', split_axis=1, concat_axis=0, tiled=True)]
    all_gather x1 -> x0, blocking collectives: 12.4 us -> none  [per_device(): lax.all_gather(context, 'inner', axis=0, tiled=True)]
  transfers between devices with their start and end apart: 9 -> 0, of which waited for: 8 -> 0; matrix products, arithmetic and copies ran while one was open for 3% -> 0% of each run, Pallas kernels for 0% -> 0%
where the time goes in v1:
time: 190 us; the launch traced here: 187 us
  Pallas kernels  184 us (97%)
  local copies, waits for them, and re-layouts  2.26 us (1%)
    pallas_call x1, Pallas kernels, per_device(): pl.pallas_call(kernel, out_shape=(jax.ShapeDtypeStruct((128, 512), BF), j...  184 us

profile of v1, /device:TPU:1, one launch (start us, length us, event | category | flops | bytes accessed | tf_op | source)
XLA Modules:
  0.0 186.8 jit_solution(10291698697757374987)
XLA Ops:
  0.6 183.8 %shard_map.104 = (bf16[128,512]{1,0:T(8,128)(2,1)}, bf16[64,1024]{1,0:T(8,128)(2,1)}) custom-call(bf16[16,4096]{1,0:T(8,128)(2,1)} %q_ref.1, bf16[16,1024]{1,0:T(8,128)(2,1)} %k_ref.1, bf16[16,1024]{1,0:T(8,128)(2,1)} %v_ref.1, s32[24]{0:T(128)} %docs_ref.1, bf16[512,1024]{1,0:T(8,128)(2,1)} %resid_ref.1, f32[8,128]{1,0:T(8,128)} %bitcast.5, ...), custom_call_target="tpu_custom_call" | custom-call | flops 4000000000 | bytes 4000000 | tf_op jit(solution)/shard_map/pallas_call | solution.py:475
  184.5 0.0 copy-start
  184.5 1.6 copy.13
  186.1 0.0 copy-done
  186.1 0.7 copy.14
Async XLA Ops:
  184.5 1.6 copy-start

commit v2 on v1

v2 whole, which is shorter than its diff:
```python
import jax
import jax.numpy as jnp
from jax import lax
from jax.experimental import pallas as pl
from jax.experimental.pallas import tpu as pltpu
from jax.sharding import PartitionSpec as P

MESH = pl.DeviceIdType.MESH
D = 4096
BF = jnp.bfloat16
F32 = jnp.float32
SCALE = 128 ** (-0.5)
DOCS = 24
NX, NY, NZ = 4, 8, 8
BACK = 5


def nt(a, b):
    return lax.dot_general(a, b, (((1,), (1,)), ((), ())), preferred_element_type=F32)


def kernel(
    q_ref, k_ref, v_ref, docs_ref, resid_ref, gain_ref, wo_ref, wgu_ref, wd_ref,
    ctx_ref, out_ref,
    q_all, keys_all, values_near, values_far, relay, scores, ctx_all, wo_all, w_all, res, gains,
    proj, proj_in, hid, acc, act, down, x_in, x_sum, y_in, rings, odd_sum, odd_in,
    send_sem, recv_sem, local_sem,
):
    head = lax.axis_index("head")
    y_lo = lax.axis_index("inner")
    outer = lax.axis_index("outer")
    x, c = head // 2, head % 2
    u, pair, mirror = x % 2, x + 1 - 2 * (x % 2), 3 - x
    y_hi, z = outer // NZ, outer % NZ
    y = y_hi * 4 + y_lo
    other = 1 - c

    def to_head(h):
        return {"head": h}

    def to_x(i):
        return {"head": i * 2 + c}

    def to_y(i):
        return {"inner": i % 4, "outer": (i // 4) * NZ + z}

    def to_z(i):
        return {"outer": y_hi * NZ + i}

    def to_outer(i):
        return {"outer": i}

    def to_lo(i):
        return {"inner": i}

    sibling = to_head(x * 2 + other)

    def feat(i):
        return (i % 4) * 2 + i // 4

    counter = [0]
    sends, locals_ = [], []

    def new(count=1):
        counter[0] += count
        return counter[0] - count

    def remote(src, dst, sid, dev):
        return pltpu.make_async_remote_copy(
            src_ref=src, dst_ref=dst, send_sem=send_sem.at[sid], recv_sem=recv_sem.at[sid],
            device_id=dev, device_id_type=MESH,
        )

    def push(src, dst, sid, dev):
        copy = remote(src, dst, sid, dev)
        copy.start()
        sends.append(copy)

    def arrive(dst, sid):
        remote(dst, dst, sid, sibling).wait_recv()

    local_count = [0]

    def local(src, dst):
        copy = pltpu.make_async_copy(src, dst, local_sem.at[local_count[0]])
        local_count[0] += 1
        copy.start()
        return copy

    def ring(n, me, to, chunk, half, arrived=None):
        steps = n // 2
        sr, sl = new(steps), new(steps)
        right, left = to((me + 1) % n), to((me + n - 1) % n)

        def run():
            for s in range(steps):
                back, ahead = (me - s + n) % n, (me + s) % n
                if s > 0:
                    arrive(chunk(back), sr + s - 1)
                    arrive(chunk(ahead), sl + s - 1)
                if s < steps - 1:
                    push(chunk(back), chunk(back), sr + s, right)
                    push(chunk(ahead), chunk(ahead), sl + s, left)
                else:
                    push(half(back, 0), half(back, 0), sr + s, right)
                    push(half(ahead, 1), half(ahead, 1), sl + s, left)
                if arrived is not None:
                    arrived(back, 2 * s)
                    if s > 0:
                        arrived(ahead, 2 * s - 1)
                yield
            far = (me + steps) % n
            arrive(half(far, 0), sr + steps - 1)
            arrive(half(far, 1), sl + steps - 1)
            if arrived is not None:
                arrived(far, 2 * steps - 1)

        return run()

    def finish(gen):
        for _ in gen:
            pass

    def together(gens):
        for _ in range(5):
            for gen in gens:
                next(gen, None)

    def lanes(core, width):
        return pl.ds(pl.multiple_of(core * width, width), width)

    barrier = pltpu.get_barrier_semaphore()
    for k in range(1, 8):
        pl.semaphore_signal(barrier, inc=1, device_id=to_head((head + k) % 8), device_id_type=MESH)
        pl.semaphore_signal(barrier, inc=1, device_id=to_y((y + k) % NY), device_id_type=MESH)
    for k in range(1, BACK):
        for peer in ((outer + k) % 16, (outer + 16 - k) % 16):
            pl.semaphore_signal(barrier, inc=1, device_id=to_outer(peer), device_id_type=MESH)
        pl.semaphore_signal(barrier, inc=1, device_id=to_z((z + k) % NZ), device_id_type=MESH)
        pl.semaphore_signal(barrier, inc=1, device_id=to_z((z + NZ - k) % NZ), device_id_type=MESH)
    pl.semaphore_wait(barrier, 30)

    kv_sid, q_sid = new(16), new(8)
    for k in range(1, 8):
        peer = (head + k) % 8
        cols = pl.ds(pl.multiple_of(peer * 128, 128), 128)
        push(k_ref.at[:, cols], keys_all.at[0, y_lo, head], kv_sid + k, to_head(peer))
        push(v_ref.at[:, cols], values_near.at[y, head], kv_sid + 8 + k, to_head(peer))
    own = pl.ds(pl.multiple_of(head * 128, 128), 128)
    keys_all[0, y_lo, head] = k_ref[:, own]
    values_near[y, head] = v_ref[:, own]
    for k in range(1, 8):
        peer = (head + k) % 8
        cols = pl.ds(pl.multiple_of(peer * 512, 512), 512)
        push(q_ref.at[:, cols], q_all.at[head], q_sid + k, to_head(peer))
    q_all[head] = q_ref[:, pl.ds(pl.multiple_of(head * 512, 512), 512)]

    w_sid = new(24)

    def w_cols(part, s):
        return pl.ds(pl.multiple_of(s * 768 + part * 128, 128), 128)

    def w_sources(i):
        cols = pl.ds(pl.multiple_of(i * 128, 128), 128)
        return wgu_ref.at[0, :, cols], wgu_ref.at[1, :, cols], wd_ref.at[:, cols]

    def w_exchange(parts):
        for k in range(1, NY):
            peer = (y + k) % NY

            @pl.when(peer != NY - 1)
            def _(k=k, peer=peer):
                for part in parts:
                    remote(
                        w_sources(peer)[part], w_all.at[feat(y), z, :, w_cols(part, c)],
                        w_sid + 3 * k + part, to_y(peer),
                    ).start()

    def w_own(part):
        return pltpu.make_async_copy(
            w_sources(y)[part], w_all.at[feat(y), z, :, w_cols(part, c)], local_sem.at[8 + part]
        )

    def w_exchanged(parts):
        @pl.when(y != NY - 1)
        def _():
            for part in parts:
                w_own(part).wait()
                for k in range(1, NY):
                    dst = w_all.at[feat((y + NY - k) % NY), z, :, w_cols(part, c)]
                    arrive(dst, w_sid + 3 * k + part)

    @pl.when(y != NY - 1)
    def _():
        for part in range(3):
            w_own(part).start()

    @pl.when(y == NY - 1)
    def _():
        def zero(f, _):
            w_all[f, z, :, pl.ds(pl.multiple_of(c * 768, 128), 384)] = jnp.zeros((64, 384), BF)
            return 0

        lax.fori_loop(0, 8, zero, 0)

    w_exchange([2])

    for k in range(1, 8):
        peer = (head + 8 - k) % 8
        arrive(keys_all.at[0, y_lo, peer], kv_sid + k)
        arrive(values_near.at[y, peer], kv_sid + 8 + k)

    def shared_ring(buf_chunk, buf_half, then=None):
        sid = new(8)

        def arrived(i, n):
            push(buf_chunk(i, c), buf_chunk(i, c), sid + n, sibling)
            if then is not None:
                then(i, n)

        gen = ring(
            NZ, z, to_z, lambda i: buf_chunk(i, c), lambda i, b: buf_half(i, b, c), arrived
        )

        def wait_sibling():
            for n in range(8):
                step = (n + 1) // 2
                i = (z + step) % NZ if n % 2 else (z - step + NZ) % NZ
                arrive(buf_chunk(i, other), sid + n)

        return gen, wait_sibling

    wo_copy = local(wo_ref, wo_all.at[z, :, lanes(c, 512)])
    wo_ring, wo_wait = shared_ring(
        lambda i, s: wo_all.at[i, :, lanes(s, 512)],
        lambda i, b, s: wo_all.at[i, pl.ds(b * 32, 32), lanes(s, 512)],
    )

    ahead_sid, key_sid, near_sid, far_sid = new(BACK), new(4 * BACK), new(8), new(BACK + 1)

    def key_lo(dz):
        for k in range(1, 4):
            push(keys_all.at[dz, y_lo], keys_all.at[dz, y_lo], key_sid + 4 * dz + k, to_lo((y_lo + k) % 4))

    for k in range(1, NY):
        push(values_near.at[y], values_near.at[y], near_sid + k, to_y((y + k) % NY))
    for dz in range(1, BACK):
        push(keys_all.at[0, y_lo], keys_all.at[dz, y_lo], ahead_sid + dz, to_outer((outer + dz) % 16))
    key_lo(0)
    wo_copy.wait()
    next(wo_ring)
    for k in range(1, NY):
        arrive(values_near.at[(y + NY - k) % NY], near_sid + k)

    def row_blocks(dz):
        return values_near.at[pl.ds(jnp.where(z + dz < NZ, y_hi, 1 - y_hi) * 4, 4)]

    push(row_blocks(4), relay, far_sid, to_z((z + NZ - 2) % NZ))
    for dz in range(1, 4):
        push(row_blocks(dz), values_far.at[dz - 1], far_sid + dz, to_z((z + dz) % NZ))
    for dz in range(1, 3):
        arrive(keys_all.at[dz, y_lo], ahead_sid + dz)
        key_lo(dz)
    next(wo_ring)
    arrive(relay, far_sid)
    push(relay, values_far.at[3], far_sid + 4, to_z((z + NZ - 2) % NZ))
    for dz in range(3, BACK):
        arrive(keys_all.at[dz, y_lo], ahead_sid + dz)
        key_lo(dz)
    w_exchange([0, 1])

    res_rows = pl.ds(pl.multiple_of(head * 64, 64), 64)
    res_sid = new()
    push(
        resid_ref.at[res_rows, lanes(1 - y_hi, 512)], res.at[y_hi], res_sid,
        to_y((1 - y_hi) * 4 + y_lo),
    )
    res_copy = local(resid_ref.at[res_rows, lanes(y_hi, 512)], res.at[y_hi])
    gain_sid = new(4)
    for k in range(1, 4):
        push(gain_ref, gains.at[y_lo], gain_sid + k, to_y(y_hi * 4 + (y_lo + k) % 4))
    gains[y_lo] = gain_ref[...]

    def w_part(i, s, first, width):
        return w_all.at[:, i, :, pl.ds(pl.multiple_of(s * 768 + first, 128), width)]

    over_sid, mirror_sid, w_core_sid = new(), new(8), new(8)
    to_mirror = to_x(mirror)
    w_exchanged([2])
    push(w_part(z, c, 256, 128), w_part(z, c, 384, 128), over_sid, to_mirror)
    next(wo_ring)
    next(wo_ring)
    for dz in range(1, BACK):
        arrive(values_far.at[dz - 1], far_sid + dz)
    for dz in range(BACK):
        for k in range(1, 4):
            arrive(keys_all.at[dz, (y_lo + 4 - k) % 4], key_sid + 4 * dz + k)

    for k in range(1, 8):
        arrive(q_all.at[(head + 8 - k) % 8], q_sid + k)
    place = outer * 512 + y_lo * 128 + lax.broadcasted_iota(jnp.int32, (128, 1), 0)
    start = jnp.zeros((128, 1), jnp.int32)
    bound = jnp.int32(0)
    for j in range(DOCS):
        bound = bound + docs_ref[j]
        start = jnp.where(bound <= place, bound, start)
    for dz in range(BACK):
        keys = keys_all[dz].reshape(512, 128)
        key_place = (outer - dz) * 512 + lax.broadcasted_iota(jnp.int32, (1, 512), 1)
        bias = jnp.where((key_place <= place) & (key_place >= start), 0.0, -1e30)
        for g in range(4):
            heads_q = q_all[:, :, g * 128:(g + 1) * 128].reshape(128, 128)
            scores[g, :, dz * 512:(dz + 1) * 512] = nt(heads_q, keys) * SCALE + bias
    for g in range(4):
        s = scores[g]
        e = jnp.exp(s - jnp.max(s, axis=1, keepdims=True))
        total = jnp.sum(e, axis=1, keepdims=True)
        e = e.astype(BF)
        summed = jnp.zeros((128, 128), F32)
        for dz in range(BACK):
            values = (values_near[pl.ds(y_hi * 4, 4)] if dz == 0 else values_far[dz - 1]).reshape(512, 128)
            summed += jnp.dot(e[:, dz * 512:(dz + 1) * 512], values, preferred_element_type=F32)
        ctx_ref[:, g * 128:(g + 1) * 128] = (summed / total).astype(BF)

    def half_rows(i):
        return pl.ds(pl.multiple_of(i * 64, 64), 64)

    ctx_sid = new()
    push(ctx_ref.at[half_rows(other)], ctx_all.at[y, :, lanes(c, 512)], ctx_sid, sibling)
    ctx_all[y, :, lanes(c, 512)] = ctx_ref[half_rows(c), :]

    w_exchanged([0, 1])
    arrive(w_part(z, c, 384, 128), over_sid)

    def w_arrived(i, n):
        push(w_part(i, c, 0, 256), w_part(i, c, 512, 256), mirror_sid + n, to_mirror)

    w_ring, w_wait = shared_ring(
        lambda i, s: w_part(i, s, 0, 512),
        lambda i, b, s: w_all.at[pl.ds(b * 4, 4), i, :, pl.ds(pl.multiple_of(s * 768, 128), 512)],
        w_arrived,
    )
    next(w_ring)

    def w_place(n):
        step = (n + 1) // 2
        return (z + step) % NZ if n % 2 else (z - step + NZ) % NZ

    def w_mirrored(*which):
        for n in which:
            gate_up_part = w_part(w_place(n), c, 512, 256)
            arrive(gate_up_part, mirror_sid + n)
            push(gate_up_part, gate_up_part, w_core_sid + n, sibling)

    arrive(ctx_all.at[y, :, lanes(other, 512)], ctx_sid)
    proj_sid = new(8)

    def proj_push(i):
        way = (i % 4 + NX - x) % NX
        return remote(
            proj.at[i], proj_in.at[way, i // 4], proj_sid + way * 2 + i // 4, to_x(i % 4)
        )

    def project(i, n):
        proj[i] = nt(ctx_all[i], wo_all[...].reshape(512, 1024)).astype(BF)

        @pl.when(i % 4 != x)
        def _():
            proj_push(i).start()

    finish(wo_ring)
    wo_wait()
    together([
        ring(
            NY, y, to_y, lambda i, p=p: ctx_all.at[i, pl.ds(p * 32, 32)],
            lambda i, b, p=p: ctx_all.at[i, pl.ds(p * 32 + b * 16, 16)],
            project if p else None,
        )
        for p in range(2)
    ])
    next(w_ring)
    w_mirrored(0)
    res_copy.wait()
    arrive(res.at[1 - y_hi], res_sid)
    for k in range(1, NX):
        for g in range(2):
            arrive(proj_in.at[k, g], proj_sid + 2 * k + g)
    for g in range(2):
        total = proj[g * 4 + x].astype(F32)
        for k in range(1, NX):
            total += proj_in[k, g].astype(F32)
        hid[feat(y), g, u] = (res[g].astype(F32) + total).astype(BF)

    first_sid, second_sid = new(), new(8)
    to_pair = to_x(pair)

    def along_x(i, n):
        push(hid.at[feat(i), 1, u], hid.at[feat(i), 1, u], second_sid + n, to_pair)

    push(hid.at[feat(y), 0, u], hid.at[feat(y), 0, u], first_sid, to_pair)
    y_first = ring(
        NY, y, to_y, lambda i: hid.at[feat(i), 1, u],
        lambda i, b: hid.at[feat(i), 1, u, pl.ds(b * 32, 32)], along_x,
    )
    next(y_first)
    arrive(hid.at[feat(y), 0, 1 - u], first_sid)
    x_first = [
        ring(
            NY, y, to_y, lambda i, p=p: hid.at[feat(i), 0, p],
            lambda i, b, p=p: hid.at[feat(i), 0, p, pl.ds(b * 32, 32)],
        )
        for p in range(2)
    ]
    for s in range(4):
        next(x_first[0])
        next(x_first[1])
        next(y_first, None)
        if s in (0, 2):
            next(w_ring)
            w_mirrored(*((1, 2) if s == 0 else (3, 4)))
    for gen in x_first:
        next(gen, None)
    for n in range(8):
        step = (n + 1) // 2
        i = (y + step) % NY if n % 2 else (y - step + NY) % NY
        arrive(hid.at[feat(i), 1, 1 - u], second_sid + n)
    finish(w_ring)
    w_mirrored(5, 6, 7)
    for n in range(8):
        arrive(w_part(w_place(n), other, 512, 256), w_core_sid + n)
    for k in range(1, 4):
        arrive(gains.at[(y_lo + 4 - k) % 4], gain_sid + k)
    w_wait()

    acc[...] = jnp.zeros_like(acc)

    def gate_up(f, squares):
        gain_row = gains[f // 2]
        rows = hid[f].reshape(256, 512).astype(F32)
        scaled = jnp.concatenate(
            [
                rows[:, j * 128:(j + 1) * 128]
                * jnp.where(f % 2 == 0, gain_row[j:j + 1], gain_row[4 + j:5 + j])
                for j in range(4)
            ],
            axis=1,
        ).astype(BF)
        for s, first in enumerate(SLOTS):
            weights = w_all[f, :, :, first:first + 256].reshape(512, 256)
            acc[s] += jnp.dot(scaled, weights, preferred_element_type=F32)
        return squares + jnp.sum(rows * rows, axis=1, keepdims=True)

    squares = lax.fori_loop(0, 8, gate_up, jnp.zeros((256, 1), F32))
    inverse = lax.rsqrt(squares / D + 1e-05)
    for s in range(4):
        gate, up = acc[s, :, :128] * inverse, acc[s, :, 128:] * inverse
        act[:, s * 128:(s + 1) * 128] = (gate / (1.0 + jnp.exp(-gate)) * up).astype(BF)

    def project_down(f, _):
        weights = jnp.concatenate(
            [w_all[f, :, :, s * 768 + 256:s * 768 + 512].reshape(512, 256) for s in range(2)], axis=1
        )
        down[f // 2, f % 2] = nt(act[...], weights).astype(BF).reshape(2, 2, 64, 512)
        return 0

    lax.fori_loop(0, 8, project_down, 0)

    ring_sid, x_sid, y_sid, odd_sid = new(16), new(4), new(8), new()
    for k in range(4):
        piece = down.at[(y_lo + k) % 4, 0, :, 1 - u]
        push(piece, x_in.at[k], x_sid + k, to_pair)

    def odd(i, p, first, count):
        return down.at[i % 4, 1, i // 4, p, pl.ds(first, count)]

    def add_even(k):
        arrive(x_in.at[k], x_sid + k)
        for g in range(2):
            mine = down[(y_lo + k) % 4, 0, g, u]
            x_sum[k, g] = (mine.astype(F32) + x_in[k, g].astype(F32)).astype(BF)
        for way in (k, k + 4):
            if way > 0:
                peer = (y + way) % NY
                push(x_sum.at[k, peer // 4], y_in.at[way - 1], y_sid + way, to_y(peer))

    to_right, to_left = to_y((y + 1) % NY), to_y((y + NY - 1) % NY)
    for s in range(4):
        for p in range(2):
            for way in range(2):
                slots, sid = rings.at[way, p], ring_sid + 8 * way + 4 * p
                i = (y + 4 - s) % NY if way == 0 else (y + 4 + s) % NY
                dev = to_right if way == 0 else to_left
                half = pl.ds(32 * way, 32)
                if s == 0:
                    push(odd(i, p, 32 * way, 32), slots.at[0, half], sid, dev)
                    continue
                if s == 1:
                    rest = pl.ds(32 * (1 - way), 32)
                    arrive(slots.at[0, half], sid)
                    slots[0, half] = (slots[0, half].astype(F32) + odd(i, p, 32 * way, 32)[...].astype(F32)).astype(BF)
                    slots[0, rest] = odd(i, p, 32 * (1 - way), 32)[...]
                else:
                    arrive(slots.at[s - 1], sid + s - 1)
                    slots[s - 1] = (slots[s - 1].astype(F32) + odd(i, p, 0, 64)[...].astype(F32)).astype(BF)
                push(slots.at[s - 1], slots.at[s], sid + s, dev)
        add_even(s)
    for p in range(2):
        total = odd(y, p, 0, 64)[...].astype(F32)
        for way in range(2):
            sid = ring_sid + 8 * way + 4 * p + 3
            arrive(rings.at[way, p, 3], sid)
            total += rings[way, p, 3].astype(F32)
        odd_sum[p] = total.astype(BF)
    push(odd_sum.at[1 - u], odd_in, odd_sid, to_pair)

    total = x_sum[0, y_hi].astype(F32)
    for k in range(1, NY):
        arrive(y_in.at[k - 1], y_sid + k)
        total += y_in[k - 1].astype(F32)
    out_ref[:, :512] = (hid[2 * y_lo, y_hi, u].astype(F32) + total).astype(BF)
    arrive(odd_in, odd_sid)
    total = odd_sum[u].astype(F32) + odd_in[...].astype(F32)
    out_ref[:, 512:] = (hid[2 * y_lo + 1, y_hi, u].astype(F32) + total).astype(BF)

    for copy in sends:
        copy.wait_send()
    for i in range(NY):
        @pl.when(i % 4 != x)
        def _(i=i):
            proj_push(i).wait_send()

    for k in range(1, NY):
        peer = (y + k) % NY

        @pl.when(peer != NY - 1)
        def _(k=k, peer=peer):
            for part, src in enumerate(w_sources(peer)):
                remote(
                    src, w_all.at[feat(y), z, :, w_cols(part, c)], w_sid + 3 * k + part, to_y(peer)
                ).wait_send()

    assert counter[0] <= SEMS, counter[0]


SEMS = 320
SLOTS = (0, 512, 768, 1280)


def per_device(query, key, value, doc_lengths, resid, norm_gain, w_out, w_gate_up, w_down):
    vmem = pl.BlockSpec(memory_space=pltpu.VMEM)
    anywhere = pl.BlockSpec(memory_space=pl.ANY)
    smem = pl.BlockSpec(memory_space=pltpu.SMEM)

    def buf(*shape, kind=BF):
        return pltpu.VMEM(shape, kind)

    return pl.pallas_call(
        kernel,
        out_shape=(
            jax.ShapeDtypeStruct((128, 512), BF),
            jax.ShapeDtypeStruct((64, 1024), BF),
        ),
        in_specs=[vmem, vmem, vmem, smem, anywhere, vmem, anywhere, anywhere, anywhere],
        out_specs=(vmem, vmem),
        scratch_shapes=[
            buf(8, 16, 512),
            buf(BACK, 4, 8, 16, 128),
            buf(8, 8, 16, 128),
            buf(BACK - 1, 4, 8, 16, 128),
            buf(4, 8, 16, 128),
            buf(4, 128, BACK * 512, kind=F32),
            buf(8, 64, 1024),
            buf(8, 64, 1024),
            buf(8, 8, 64, 1536),
            buf(2, 64, 512),
            buf(4, 8, 128, kind=F32),
            buf(8, 64, 512),
            buf(4, 2, 64, 512),
            buf(8, 2, 2, 64, 512),
            buf(4, 256, 256, kind=F32),
            buf(256, 512),
            buf(4, 2, 2, 2, 64, 512),
            buf(4, 2, 64, 512),
            buf(4, 2, 64, 512),
            buf(7, 64, 512),
            buf(2, 2, 4, 64, 512),
            buf(2, 64, 512),
            buf(64, 512),
            pltpu.SemaphoreType.DMA((SEMS,)),
            pltpu.SemaphoreType.DMA((SEMS,)),
            pltpu.SemaphoreType.DMA((16,)),
        ],
        compiler_params=pltpu.CompilerParams(
            collective_id=0, has_side_effects=True, vmem_limit_bytes=56 * 1024 * 1024
        ),
        cost_estimate=pl.CostEstimate(flops=4_000_000_000, bytes_accessed=4_000_000, transcendentals=2_000_000),
    )(
        query, key, value, doc_lengths, resid, norm_gain.reshape(8, 128),
        w_out.T, w_gate_up, w_down.T,
    )


def solution(mesh):
    placed = (
        P(("outer", "inner", "head"), None),
        P(("outer", "inner", "head"), None),
        P(("outer", "inner", "head"), None),
        P(),
        P("outer", "inner"),
        P("inner"),
        P("head", ("inner", "outer")),
        P(None, ("inner", "outer"), "head"),
        P("head", ("inner", "outer")),
    )
    return jax.shard_map(
        per_device,
        mesh=mesh,
        in_specs=placed,
        out_specs=(P(("outer", "inner"), "head"), P(("outer", "head"), "inner")),
        check_vma=False,
    )
```

time: 190 us -> 166 us (0.87); the launches traced: 187 us -> 166 us
  Pallas kernels: 184 us -> 163 us
    pallas_call x1, Pallas kernels: 184 us -> 163 us  [per_device(): pl.pallas_call(kernel, out_shape=(jax.ShapeDtypeStruct((128, 512), BF), j...]
where the time goes in v2:
time: 166 us
  Pallas kernels  163 us (98%)
  local copies, waits for them, and re-layouts  2.26 us (1%)
    pallas_call x1, Pallas kernels, per_device(): pl.pallas_call(kernel, out_shape=(jax.ShapeDtypeStruct((128, 512), BF), j...  163 us

profile of v2, /device:TPU:1, one launch (start us, length us, event | category | flops | bytes accessed | tf_op | source)
XLA Modules:
  0.0 166.3 jit_solution(13459924364170020096)
XLA Ops:
  0.6 163.4 %shard_map.104 = (bf16[128,512]{1,0:T(8,128)(2,1)}, bf16[64,1024]{1,0:T(8,128)(2,1)}) custom-call(bf16[16,4096]{1,0:T(8,128)(2,1)} %q_ref.1, bf16[16,1024]{1,0:T(8,128)(2,1)} %k_ref.1, bf16[16,1024]{1,0:T(8,128)(2,1)} %v_ref.1, s32[24]{0:T(128)} %docs_ref.1, bf16[512,1024]{1,0:T(8,128)(2,1)} %resid_ref.1, f32[8,128]{1,0:T(8,128)} %bitcast.5, ...), custom_call_target="tpu_custom_call" | custom-call | flops 4000000000 | bytes 4000000 | tf_op jit(solution)/shard_map/pallas_call | solution.py:557
  164.0 0.0 copy-start
  164.0 1.6 copy.13
  165.6 0.0 copy-done
  165.6 0.7 copy.14
Async XLA Ops:
  164.0 1.6 copy-start

commit v3 on v2

v3 whole, which is shorter than its diff:
```python
import jax
import jax.numpy as jnp
from jax import lax
from jax.experimental import pallas as pl
from jax.experimental.pallas import tpu as pltpu
from jax.sharding import PartitionSpec as P

MESH = pl.DeviceIdType.MESH
D = 4096
BF = jnp.bfloat16
F32 = jnp.float32
SCALE = 128 ** (-0.5)
DOCS = 24
NX, NY, NZ = 4, 8, 8
BACK = 5


def nt(a, b):
    return lax.dot_general(a, b, (((1,), (1,)), ((), ())), preferred_element_type=F32)


def kernel(
    q_ref, k_ref, v_ref, docs_ref, resid_ref, gain_ref, wo_ref, wgu_ref, wd_ref,
    ctx_ref, out_ref,
    q_all, keys_all, values_near, values_far, relay, scores, ctx_all, wo_all, w_all, res, gains,
    proj, proj_in, hid, acc, act, down, x_in, x_sum, rings, odd_sum, odd_in,
    send_sem, recv_sem, local_sem,
):
    head = lax.axis_index("head")
    y_lo = lax.axis_index("inner")
    outer = lax.axis_index("outer")
    x, c = head // 2, head % 2
    u, pair, mirror = x % 2, x + 1 - 2 * (x % 2), 3 - x
    y_hi, z = outer // NZ, outer % NZ
    y = y_hi * 4 + y_lo
    other = 1 - c

    def to_head(h):
        return {"head": h}

    def to_x(i):
        return {"head": i * 2 + c}

    def to_y(i):
        return {"inner": i % 4, "outer": (i // 4) * NZ + z}

    def to_z(i):
        return {"outer": y_hi * NZ + i}

    def to_outer(i):
        return {"outer": i}

    def to_lo(i):
        return {"inner": i}

    def to_cross(i):
        return {"head": x * 2 + other, "inner": i}

    sibling = to_head(x * 2 + other)

    def feat(i):
        return (i % 4) * 2 + i // 4

    counter = [0]
    sends, locals_ = [], []

    def new(count=1):
        counter[0] += count
        return counter[0] - count

    def remote(src, dst, sid, dev):
        return pltpu.make_async_remote_copy(
            src_ref=src, dst_ref=dst, send_sem=send_sem.at[sid], recv_sem=recv_sem.at[sid],
            device_id=dev, device_id_type=MESH,
        )

    def push(src, dst, sid, dev):
        copy = remote(src, dst, sid, dev)
        copy.start()
        sends.append(copy)

    maybes = []

    def push_if(cond, *args):
        @pl.when(cond)
        def _():
            remote(*args).start()

        maybes.append((cond, args))

    def arrive_if(cond, *args):
        @pl.when(cond)
        def _():
            arrive(*args)

    def arrive(dst, sid):
        remote(dst, dst, sid, sibling).wait_recv()

    local_count = [0]

    def local(src, dst):
        copy = pltpu.make_async_copy(src, dst, local_sem.at[local_count[0]])
        local_count[0] += 1
        copy.start()
        return copy

    def ring(n, me, to, chunk, half, arrived=None):
        steps = n // 2
        sr, sl = new(steps), new(steps)
        right, left = to((me + 1) % n), to((me + n - 1) % n)

        def run():
            for s in range(steps):
                back, ahead = (me - s + n) % n, (me + s) % n
                if s > 0:
                    arrive(chunk(back), sr + s - 1)
                    arrive(chunk(ahead), sl + s - 1)
                if s < steps - 1:
                    push(chunk(back), chunk(back), sr + s, right)
                    push(chunk(ahead), chunk(ahead), sl + s, left)
                elif half is None:
                    push(chunk(ahead), chunk(ahead), sl + s, left)
                else:
                    push(half(back, 0), half(back, 0), sr + s, right)
                    push(half(ahead, 1), half(ahead, 1), sl + s, left)
                if arrived is not None:
                    arrived(back, 2 * s)
                    if s > 0:
                        arrived(ahead, 2 * s - 1)
                yield
            far = (me + steps) % n
            if half is None:
                arrive(chunk(far), sl + steps - 1)
            else:
                arrive(half(far, 0), sr + steps - 1)
                arrive(half(far, 1), sl + steps - 1)
            if arrived is not None:
                arrived(far, 2 * steps - 1)

        return run()

    def finish(gen):
        for _ in gen:
            pass

    def together(gens):
        for _ in range(5):
            for gen in gens:
                next(gen, None)

    def lanes(core, width):
        return pl.ds(pl.multiple_of(core * width, width), width)

    keys_all[...] = jnp.zeros_like(keys_all)
    values_near[...] = jnp.zeros_like(values_near)

    barrier = pltpu.get_barrier_semaphore()
    for k in range(1, 8):
        pl.semaphore_signal(barrier, inc=1, device_id=to_head((head + k) % 8), device_id_type=MESH)
        pl.semaphore_signal(barrier, inc=1, device_id=to_y((y + k) % NY), device_id_type=MESH)
    for k in range(1, BACK):
        for peer in ((outer + k) % 16, (outer + 16 - k) % 16):
            pl.semaphore_signal(barrier, inc=1, device_id=to_outer(peer), device_id_type=MESH)
        pl.semaphore_signal(barrier, inc=1, device_id=to_z((z + k) % NZ), device_id_type=MESH)
        pl.semaphore_signal(barrier, inc=1, device_id=to_z((z + NZ - k) % NZ), device_id_type=MESH)
    for k in range(1, 4):
        pl.semaphore_signal(barrier, inc=1, device_id=to_cross((y_lo + k) % 4), device_id_type=MESH)
    pl.semaphore_wait(barrier, 33)

    kv_sid, q_sid = new(16), new(8)
    for k in range(1, 8):
        peer = (head + k) % 8
        cols = pl.ds(pl.multiple_of(peer * 128, 128), 128)
        push(k_ref.at[:, cols], keys_all.at[0, y_lo, head], kv_sid + k, to_head(peer))
        push(v_ref.at[:, cols], values_near.at[y, head], kv_sid + 8 + k, to_head(peer))
    own = pl.ds(pl.multiple_of(head * 128, 128), 128)
    own_copies = [
        local(k_ref.at[:, own], keys_all.at[0, y_lo, head]),
        local(v_ref.at[:, own], values_near.at[y, head]),
    ]
    for k in range(1, 8):
        peer = (head + k) % 8
        cols = pl.ds(pl.multiple_of(peer * 512, 512), 512)
        push(q_ref.at[:, cols], q_all.at[head], q_sid + k, to_head(peer))
    own_copies.append(local(q_ref.at[:, pl.ds(pl.multiple_of(head * 512, 512), 512)], q_all.at[head]))

    w_sid = new(24)

    def w_cols(part, s):
        return pl.ds(pl.multiple_of(s * 768 + part * 128, 128), 128)

    def w_sources(i):
        cols = pl.ds(pl.multiple_of(i * 128, 128), 128)
        return wgu_ref.at[0, :, cols], wgu_ref.at[1, :, cols], wd_ref.at[:, cols]

    def w_exchange(parts):
        for k in range(1, NY):
            peer = (y + k) % NY

            @pl.when(peer != NY - 1)
            def _(k=k, peer=peer):
                for part in parts:
                    remote(
                        w_sources(peer)[part], w_all.at[feat(y), z, :, w_cols(part, c)],
                        w_sid + 3 * k + part, to_y(peer),
                    ).start()

    def w_own(part):
        return pltpu.make_async_copy(
            w_sources(y)[part], w_all.at[feat(y), z, :, w_cols(part, c)], local_sem.at[8 + part]
        )

    def w_exchanged(parts):
        @pl.when(y != NY - 1)
        def _():
            for part in parts:
                w_own(part).wait()
                for k in range(1, NY):
                    dst = w_all.at[feat((y + NY - k) % NY), z, :, w_cols(part, c)]
                    arrive(dst, w_sid + 3 * k + part)

    @pl.when(y != NY - 1)
    def _():
        for part in range(3):
            w_own(part).start()

    @pl.when(y == NY - 1)
    def _():
        def zero(f, _):
            w_all[f, z, :, pl.ds(pl.multiple_of(c * 768, 128), 384)] = jnp.zeros((64, 384), BF)
            return 0

        lax.fori_loop(0, 8, zero, 0)

    wo_sid = new()
    push(wo_ref, wo_all.at[y_hi, z, :, lanes(c, 512)], wo_sid, to_y((1 - y_hi) * 4 + y_lo))
    wo_copy = local(wo_ref, wo_all.at[y_hi, z, :, lanes(c, 512)])
    res_copy = local(resid_ref.at[pl.ds(pl.multiple_of(head * 64, 64), 64)], res)

    for copy in own_copies:
        copy.wait()
    for k in range(1, 8):
        peer = (head + 8 - k) % 8
        arrive(keys_all.at[0, y_lo, peer], kv_sid + k)
        arrive(values_near.at[y, peer], kv_sid + 8 + k)

    def shared_ring(buf_chunk, then=None, buf_half=None):
        sid = new(8)

        def arrived(i, n):
            push(buf_chunk(i, c), buf_chunk(i, c), sid + n, sibling)
            if then is not None:
                then(i, n)

        half = None if buf_half is None else lambda i, b: buf_half(i, b, c)
        gen = ring(NZ, z, to_z, lambda i: buf_chunk(i, c), half, arrived)

        def wait_sibling():
            for n in range(8):
                step = (n + 1) // 2
                i = (z + step) % NZ if n % 2 else (z - step + NZ) % NZ
                arrive(buf_chunk(i, other), sid + n)

        return gen, wait_sibling

    wo_ring, wo_wait = shared_ring(
        lambda i, s: wo_all.at[:, i, :, lanes(s, 512)]
    )

    ahead_sid, key_sid, near_sid, far_sid = new(BACK), new(4 * BACK), new(8), new(BACK + 1)

    def key_wanted(dz, src, dst):
        seen = outer >= dz
        return seen & (src < dst) if dz == 0 else seen & (src > dst) if dz == 4 else seen

    def key_lo(dz):
        for k in range(1, 4):
            peer = (y_lo + k) % 4
            push_if(
                key_wanted(dz, y_lo, peer),
                keys_all.at[dz, y_lo], keys_all.at[dz, y_lo], key_sid + 4 * dz + k, to_lo(peer),
            )

    def key_ahead(dz):
        arrive_if(outer >= dz, keys_all.at[dz, y_lo], ahead_sid + dz)

    def near_wanted(row):
        return (row == y_hi) | ((z >= 4) & (row == 0))

    for k in range(1, NY):
        peer = (y + k) % NY
        push_if(
            (peer // 4 == y_hi) | ((z >= 4) & (y_hi == 0)),
            values_near.at[y], values_near.at[y], near_sid + k, to_y(peer),
        )
    for dz in range(1, BACK):
        push_if(
            outer + dz < 16,
            keys_all.at[0, y_lo], keys_all.at[dz, y_lo], ahead_sid + dz, to_outer((outer + dz) % 16),
        )
    key_lo(0)
    wo_copy.wait()
    arrive(wo_all.at[1 - y_hi, z, :, lanes(c, 512)], wo_sid)
    next(wo_ring)
    for k in range(1, NY):
        peer = (y + NY - k) % NY
        arrive_if(near_wanted(peer // 4), values_near.at[peer], near_sid + k)
        if k == 4:
            next(wo_ring)

    def row_blocks(dz):
        return values_near.at[pl.ds(jnp.where(z + dz < NZ, y_hi, 1 - y_hi) * 4, 4)]

    push(row_blocks(4), relay, far_sid, to_z((z + NZ - 2) % NZ))
    for dz in range(1, 3):
        push(row_blocks(dz), values_far.at[dz - 1], far_sid + dz, to_z((z + dz) % NZ))
    push_if(z == NZ - 3, row_blocks(3), values_far.at[2], far_sid + 3, to_z((z + 3) % NZ))
    w_exchange([0, 1, 2])
    for dz in range(1, 3):
        key_ahead(dz)
        key_lo(dz)
    next(wo_ring)
    arrive(values_far.at[1], far_sid + 2)
    push_if(z != NZ - 1, values_far.at[1], values_far.at[2], far_sid + 3, to_z((z + 1) % NZ))
    arrive(relay, far_sid)
    push(relay, values_far.at[3], far_sid + 4, to_z((z + NZ - 2) % NZ))
    for dz in range(3, BACK):
        key_ahead(dz)
        key_lo(dz)

    def w_part(i, s, first, width, f=0, count=8):
        return w_all.at[pl.ds(f, count), i, :, pl.ds(pl.multiple_of(s * 768 + first, 128), width)]

    over_sid, mirror_sid, w_core_sid = new(2), new(24), new(24)
    to_mirror = to_x(mirror)
    next(wo_ring)
    gain_sid = new(4)
    for k in range(1, 4):
        push(gain_ref, gains.at[y_lo], gain_sid + k, to_lo((y_lo + k) % 4))
    gains[y_lo] = gain_ref[...]
    w_exchanged([0, 1, 2])
    push(w_part(z, c, 256, 128), w_part(z, c, 384, 128), over_sid, to_mirror)
    push(w_part(z, c, 0, 256, 6, 2), w_part(z, c, 512, 256, 6, 2), over_sid + 1, to_mirror)

    def w_quarter_ring(p):
        if p == 3:
            return shared_ring(
                lambda i, s: w_part(i, s, 0, 768, 6, 2), None,
                lambda i, b, s: w_part(i, s, 0, 768, 6 + b, 1),
            )

        def w_arrived(i, n):
            push(
                w_part(i, c, 0, 256, 2 * p, 2), w_part(i, c, 512, 256, 2 * p, 2),
                mirror_sid + 8 * p + n, to_mirror,
            )

        return shared_ring(
            lambda i, s: w_part(i, s, 0, 512, 2 * p, 2), w_arrived,
            lambda i, b, s: w_part(i, s, 0, 512, 2 * p + b, 1),
        )

    w_rings = [w_quarter_ring(p) for p in range(4)]

    def w_place(n):
        step = (n + 1) // 2
        return (z + step) % NZ if n % 2 else (z - step + NZ) % NZ

    def w_step(p, *which):
        next(w_rings[p][0], None)
        for n in which if p < 3 else ():
            gate_up_part = w_part(w_place(n), c, 512, 256, 2 * p, 2)
            arrive(gate_up_part, mirror_sid + 8 * p + n)
            push(gate_up_part, gate_up_part, w_core_sid + 8 * p + n, sibling)

    arrive(w_part(z, c, 384, 128), over_sid)
    arrive(w_part(z, c, 512, 256, 6, 2), over_sid + 1)
    for p in range(4):
        w_step(p)
    for dz in (1, 3, 4):
        arrive(values_far.at[dz - 1], far_sid + dz)
    for dz in range(BACK):
        for k in range(1, 4):
            peer = (y_lo + 4 - k) % 4
            arrive_if(key_wanted(dz, peer, y_lo), keys_all.at[dz, peer], key_sid + 4 * dz + k)

    for k in range(1, 8):
        arrive(q_all.at[(head + 8 - k) % 8], q_sid + k)
    place = outer * 512 + y_lo * 128 + lax.broadcasted_iota(jnp.int32, (128, 1), 0)
    start = jnp.zeros((128, 1), jnp.int32)
    bound = jnp.int32(0)
    for j in range(DOCS):
        bound = bound + docs_ref[j]
        start = jnp.where(bound <= place, bound, start)
    for dz in range(BACK):
        keys = keys_all[dz].reshape(512, 128)
        key_place = (outer - dz) * 512 + lax.broadcasted_iota(jnp.int32, (1, 512), 1)
        bias = jnp.where((key_place <= place) & (key_place >= start), 0.0, -1e30)
        for g in range(4):
            heads_q = q_all[:, :, g * 128:(g + 1) * 128].reshape(128, 128)
            scores[g, :, dz * 512:(dz + 1) * 512] = nt(heads_q, keys) * SCALE + bias
    for g in range(4):
        s = scores[g]
        e = jnp.exp(s - jnp.max(s, axis=1, keepdims=True))
        total = jnp.sum(e, axis=1, keepdims=True)
        e = e.astype(BF)
        summed = jnp.zeros((128, 128), F32)
        for dz in range(BACK):
            values = (values_near[pl.ds(y_hi * 4, 4)] if dz == 0 else values_far[dz - 1]).reshape(512, 128)
            summed += jnp.dot(e[:, dz * 512:(dz + 1) * 512], values, preferred_element_type=F32)
        ctx_ref[:, g * 128:(g + 1) * 128] = (summed / total).astype(BF)

    def half_rows(i):
        return ctx_ref.at[pl.ds(pl.multiple_of(i * 64, 64), 64)]

    def ctx_part(i, core):
        return ctx_all.at[i, :, lanes(core, 512)]

    ctx_sid, cross_sid = new(4), new(4)
    for k in range(1, 4):
        peer = (y_lo + k) % 4
        push(half_rows(c), ctx_part(y_lo, c), ctx_sid + k, to_lo(peer))
        push(half_rows(other), ctx_part(y_lo, c), cross_sid + k, to_cross(peer))
    push(half_rows(other), ctx_part(y_lo, c), cross_sid, sibling)
    ctx_all[y_lo, :, lanes(c, 512)] = half_rows(c)[...]

    w_step(0, 0)
    w_step(1, 0)

    proj_sid = new(4)

    def proj_push(i):
        way = (i + NX - x) % NX
        return remote(proj.at[i], proj_in.at[way], proj_sid + way, to_x(i))

    finish(wo_ring)
    wo_wait()
    for k in range(4):
        i = (y_lo + 4 - k) % 4
        if k > 0:
            arrive(ctx_part(i, c), ctx_sid + k)
        arrive(ctx_part(i, other), cross_sid + k)
        proj[i] = nt(ctx_all[i], wo_all[...].reshape(1024, 1024)).astype(BF)

        @pl.when(i != x)
        def _(i=i):
            proj_push(i).start()

        if k in (1, 2):
            w_step(k + 1, 0)

    res_copy.wait()
    total = proj[x].astype(F32)
    for k in range(1, NX):
        arrive(proj_in.at[k], proj_sid + k)
        total += proj_in[k].astype(F32)
    total = (res[...].astype(F32) + total).astype(BF)
    for b in range(2):
        hid[y_lo, b, y_hi, u] = total[:, b * 512:(b + 1) * 512]
    def hid_part(i, b, p, half=None):
        part = hid.at[i % 4, b, i // 4, p]
        return part if half is None else part.at[pl.ds(half * 32, 32)]

    first_sid, second_sid = new(), new(8)
    to_pair = to_x(pair)

    def along_x(i, n):
        push(hid_part(i, 1, u), hid_part(i, 1, u), second_sid + n, to_pair)

    push(hid_part(y, 0, u), hid_part(y, 0, u), first_sid, to_pair)
    y_first = ring(
        NY, y, to_y, lambda i: hid_part(i, 1, u),
        lambda i, b: hid_part(i, 1, u, b), along_x,
    )
    next(y_first)
    w_step(0, 1, 2)
    w_step(1, 1, 2)
    arrive(hid_part(y, 0, 1 - u), first_sid)
    x_first = [
        ring(
            NY, y, to_y, lambda i, p=p: hid_part(i, 0, p),
            lambda i, b, p=p: hid_part(i, 0, p, b),
        )
        for p in range(2)
    ]
    for s in range(4):
        next(x_first[0])
        next(x_first[1])
        next(y_first, None)
        if s == 0:
            w_step(2, 1, 2)
            w_step(3, 1, 2)
        if s in (1, 2):
            w_step(2 * s - 2, 3, 4)
            w_step(2 * s - 1, 3, 4)
        if s == 3:
            w_step(0, 5, 6)
            w_step(1, 5, 6)
    for gen in x_first:
        next(gen, None)
    for n in range(8):
        step = (n + 1) // 2
        i = (y + step) % NY if n % 2 else (y - step + NY) % NY
        arrive(hid_part(i, 1, 1 - u), second_sid + n)
    for k in range(1, 4):
        arrive(gains.at[(y_lo + 4 - k) % 4], gain_sid + k)
    w_step(2, 5, 6)
    w_step(3, 5, 6)
    for p in range(4):
        w_step(p, 7)
        w_rings[p][1]()
        for n in range(8 if p < 3 else 0):
            arrive(w_part(w_place(n), other, 512, 256, 2 * p, 2), w_core_sid + 8 * p + n)

    acc[...] = jnp.zeros_like(acc)

    def gate_up(f, squares):
        gain_row = gains[f // 2]
        rows = hid[f // 2, f % 2].reshape(256, 512).astype(F32)
        scaled = jnp.concatenate(
            [
                rows[:, j * 128:(j + 1) * 128]
                * jnp.where(f % 2 == 0, gain_row[j:j + 1], gain_row[4 + j:5 + j])
                for j in range(4)
            ],
            axis=1,
        ).astype(BF)
        for s, first in enumerate(SLOTS):
            weights = w_all[f, :, :, first:first + 256].reshape(512, 256)
            acc[s] += jnp.dot(scaled, weights, preferred_element_type=F32)
        return squares + jnp.sum(rows * rows, axis=1, keepdims=True)

    squares = lax.fori_loop(0, 8, gate_up, jnp.zeros((256, 1), F32))
    inverse = lax.rsqrt(squares / D + 1e-05)
    for s in range(4):
        gate, up = acc[s, :, :128] * inverse, acc[s, :, 128:] * inverse
        act[:, s * 128:(s + 1) * 128] = (gate / (1.0 + jnp.exp(-gate)) * up).astype(BF)

    x_sid, odd_sid = new(4), new()

    def project_down(lo, b):
        f = lo * 2 + b
        weights = jnp.concatenate(
            [w_all[f, :, :, s * 768 + 256:s * 768 + 512].reshape(512, 256) for s in range(2)], axis=1
        )
        down[lo, b] = nt(act[...], weights).astype(BF).reshape(2, 2, 64, 512)

    def sum_ring(block, slots):
        sid = new(8)
        to_way = to_y((y + 1) % NY), to_y((y + NY - 1) % NY)

        def run():
            for s in range(4):
                for way in range(2):
                    buf, first_sid = slots.at[way], sid + 4 * way
                    i = (y + 4 - s) % NY if way == 0 else (y + 4 + s) % NY
                    half = pl.ds(32 * way, 32)
                    if s == 0:
                        push(block(i, 32 * way, 32), buf.at[0, half], first_sid, to_way[way])
                        continue
                    if s == 1:
                        arrive(buf.at[0, half], first_sid)
                        mine = block(i, 32 * way, 32)[...]
                        buf[0, half] = (buf[0, half].astype(F32) + mine.astype(F32)).astype(BF)
                        buf[0, pl.ds(32 * (1 - way), 32)] = block(i, 32 * (1 - way), 32)[...]
                    else:
                        arrive(buf.at[s - 1], first_sid + s - 1)
                        mine = block(i, 0, 64)[...]
                        buf[s - 1] = (buf[s - 1].astype(F32) + mine.astype(F32)).astype(BF)
                    push(buf.at[s - 1], buf.at[s], first_sid + s, to_way[way])
                yield

        def total():
            result = block(y, 0, 64)[...].astype(F32)
            for way in range(2):
                arrive(slots.at[way, 3], sid + 4 * way + 3)
                result += slots[way, 3].astype(F32)
            return result

        return run(), total

    odd_rings = [
        sum_ring(
            lambda i, first, count, p=p: down.at[i % 4, 1, i // 4, p, pl.ds(first, count)], rings.at[p]
        )
        for p in range(2)
    ]
    even_ring = sum_ring(lambda i, first, count: x_sum.at[i % 4, i // 4, pl.ds(first, count)], rings.at[2])

    def odd_step():
        for gen, _ in odd_rings:
            next(gen)

    def add_even(*pieces):
        for k in pieces:
            lo = (y_lo + k) % 4
            arrive(x_in.at[k], x_sid + k)
            for g in range(2):
                x_sum[lo, g] = (down[lo, 0, g, u].astype(F32) + x_in[k, g].astype(F32)).astype(BF)
        next(even_ring[0])

    for k in (0, 1, 3, 2):
        lo = (y_lo + k) % 4
        project_down(lo, 0)
        push(down.at[lo, 0, :, 1 - u], x_in.at[k], x_sid + k, to_pair)
    for k in (0, 1, 3, 2):
        project_down((y_lo + k) % 4, 1)
        if k == 0:
            odd_step()

    add_even(0)
    odd_step()
    add_even(1, 3)
    odd_step()
    add_even(2)
    odd_step()
    add_even()
    for p in range(2):
        odd_sum[p] = odd_rings[p][1]().astype(BF)
    push(odd_sum.at[1 - u], odd_in, odd_sid, to_pair)
    out_ref[:, :512] = (hid[y_lo, 0, y_hi, u].astype(F32) + even_ring[1]()).astype(BF)
    arrive(odd_in, odd_sid)
    total = odd_sum[u].astype(F32) + odd_in[...].astype(F32)
    out_ref[:, 512:] = (hid[y_lo, 1, y_hi, u].astype(F32) + total).astype(BF)

    for copy in sends:
        copy.wait_send()
    for cond, args in maybes:
        @pl.when(cond)
        def _(args=args):
            remote(*args).wait_send()

    for i in range(NX):
        @pl.when(i != x)
        def _(i=i):
            proj_push(i).wait_send()

    for k in range(1, NY):
        peer = (y + k) % NY

        @pl.when(peer != NY - 1)
        def _(k=k, peer=peer):
            for part, src in enumerate(w_sources(peer)):
                remote(
                    src, w_all.at[feat(y), z, :, w_cols(part, c)], w_sid + 3 * k + part, to_y(peer)
                ).wait_send()

    assert counter[0] <= SEMS, counter[0]


SEMS = 460
SLOTS = (0, 512, 768, 1280)


def per_device(query, key, value, doc_lengths, resid, norm_gain, w_out, w_gate_up, w_down):
    vmem = pl.BlockSpec(memory_space=pltpu.VMEM)
    anywhere = pl.BlockSpec(memory_space=pl.ANY)
    smem = pl.BlockSpec(memory_space=pltpu.SMEM)

    def buf(*shape, kind=BF):
        return pltpu.VMEM(shape, kind)

    return pl.pallas_call(
        kernel,
        out_shape=(
            jax.ShapeDtypeStruct((128, 512), BF),
            jax.ShapeDtypeStruct((64, 1024), BF),
        ),
        in_specs=[anywhere, anywhere, anywhere, smem, anywhere, vmem, anywhere, anywhere, anywhere],
        out_specs=(vmem, vmem),
        scratch_shapes=[
            buf(8, 16, 512),
            buf(BACK, 4, 8, 16, 128),
            buf(8, 8, 16, 128),
            buf(BACK - 1, 4, 8, 16, 128),
            buf(4, 8, 16, 128),
            buf(4, 128, BACK * 512, kind=F32),
            buf(4, 64, 1024),
            buf(2, 8, 64, 1024),
            buf(8, 8, 64, 1536),
            buf(64, 1024),
            buf(4, 8, 128, kind=F32),
            buf(4, 64, 1024),
            buf(4, 64, 1024),
            buf(4, 2, 2, 2, 64, 512),
            buf(4, 256, 256, kind=F32),
            buf(256, 512),
            buf(4, 2, 2, 2, 64, 512),
            buf(4, 2, 64, 512),
            buf(4, 2, 64, 512),
            buf(3, 2, 4, 64, 512),
            buf(2, 64, 512),
            buf(64, 512),
            pltpu.SemaphoreType.DMA((SEMS,)),
            pltpu.SemaphoreType.DMA((SEMS,)),
            pltpu.SemaphoreType.DMA((16,)),
        ],
        compiler_params=pltpu.CompilerParams(
            collective_id=0, has_side_effects=True, vmem_limit_bytes=56 * 1024 * 1024
        ),
        cost_estimate=pl.CostEstimate(flops=4_000_000_000, bytes_accessed=4_000_000, transcendentals=2_000_000),
    )(
        query, key, value, doc_lengths, resid, norm_gain.reshape(8, 128),
        w_out.T, w_gate_up, w_down.T,
    )


def solution(mesh):
    placed = (
        P(("outer", "inner", "head"), None),
        P(("outer", "inner", "head"), None),
        P(("outer", "inner", "head"), None),
        P(),
        P("outer", "inner"),
        P("inner"),
        P("head", ("inner", "outer")),
        P(None, ("inner", "outer"), "head"),
        P("head", ("inner", "outer")),
    )
    return jax.shard_map(
        per_device,
        mesh=mesh,
        in_specs=placed,
        out_specs=(P(("outer", "inner"), "head"), P(("outer", "head"), "inner")),
        check_vma=False,
    )
```

time: 166 us -> 150 us (0.904)
  Pallas kernels: 163 us -> 146 us
    pallas_call x1, Pallas kernels: 163 us -> 146 us  [per_device(): pl.pallas_call(kernel, out_shape=(jax.ShapeDtypeStruct((128, 512), BF), j...]
where the time goes in v3:
time: 150 us; the launch traced here: 149 us
  Pallas kernels  146 us (97%)
  local copies, waits for them, and re-layouts  2.26 us (2%)
    pallas_call x1, Pallas kernels, per_device(): pl.pallas_call(kernel, out_shape=(jax.ShapeDtypeStruct((128, 512), BF), j...  146 us

profile of v3, /device:TPU:1, one launch (start us, length us, event | category | flops | bytes accessed | tf_op | source)
XLA Modules:
  0.0 148.6 jit_solution(2659430243194813208)
XLA Ops:
  0.6 145.7 %shard_map.104 = (bf16[128,512]{1,0:T(8,128)(2,1)}, bf16[64,1024]{1,0:T(8,128)(2,1)}) custom-call(bf16[16,4096]{1,0:T(8,128)(2,1)} %q_ref.1, bf16[16,1024]{1,0:T(8,128)(2,1)} %k_ref.1, bf16[16,1024]{1,0:T(8,128)(2,1)} %v_ref.1, s32[24]{0:T(128)} %docs_ref.1, bf16[512,1024]{1,0:T(8,128)(2,1)} %resid_ref.1, f32[8,128]{1,0:T(8,128)} %bitcast.5, ...), custom_call_target="tpu_custom_call" | custom-call | flops 4000000000 | bytes 4000000 | tf_op jit(solution)/shard_map/pallas_call | solution.py:663
  146.3 0.0 copy-start
  146.4 1.6 %copy.13 = bf16[128,512]{1,0:T(8,128)(2,1)} copy(bf16[128,512]{1,0:T(8,128)(2,1)} %get-tuple-element.4) | data formatting | bytes 262144
  148.0 0.0 copy-done
  148.0 0.7 copy.14
Async XLA Ops:
  146.3 1.6 %copy-start = (bf16[64,1024]{1,0:T(8,128)(2,1)S(1)}, bf16[64,1024]{1,0:T(8,128)(2,1)}, u32[]{:S(2)}) copy-start(bf16[64,1024]{1,0:T(8,128)(2,1)} %get-tuple-element.5) | copy-start | bytes 393220

commit v4 on v3

--- a/solution.py
+++ b/solution.py
@@ -1,3 +1,5 @@
+import math
+
 import jax
 import jax.numpy as jnp
 from jax import lax
@@ -22,7 +24,7 @@
 def kernel(
     q_ref, k_ref, v_ref, docs_ref, resid_ref, gain_ref, wo_ref, wgu_ref, wd_ref,
     ctx_ref, out_ref,
-    q_all, keys_all, values_near, values_far, relay, scores, ctx_all, wo_all, w_all, res, gains,
+    q_all, keys_all, values_near, values_far, relay, scores, ctx_own, ctx_all, wo_all, w_all, res, gains,
     proj, proj_in, hid, acc, act, down, x_in, x_sum, rings, odd_sum, odd_in,
     send_sem, recv_sem, local_sem,
 ):
@@ -62,31 +64,38 @@
         return (i % 4) * 2 + i // 4
 
     counter = [0]
-    sends, locals_ = [], []
 
     def new(count=1):
         counter[0] += count
         return counter[0] - count
 
-    def remote(src, dst, sid, dev):
+    def remote(src, dst, sid, dev, ssid=0):
         return pltpu.make_async_remote_copy(
-            src_ref=src, dst_ref=dst, send_sem=send_sem.at[sid], recv_sem=recv_sem.at[sid],
+            src_ref=src, dst_ref=dst, send_sem=send_sem.at[ssid], recv_sem=recv_sem.at[sid],
             device_id=dev, device_id_type=MESH,
         )
 
+    sent = [0]
+
+    def count(units):
+        sent[-1] += units
+        if sent[-1] >= FULL and block_shape(sent[-1]) is not None:
+            sent.append(0)
+
     def push(src, dst, sid, dev):
-        copy = remote(src, dst, sid, dev)
-        copy.start()
-        sends.append(copy)
+        remote(src, dst, sid, dev, len(sent) - 1).start()
+        count(math.prod(src.shape) * jnp.dtype(src.dtype).itemsize // 4096)
 
     maybes = []
 
-    def push_if(cond, *args):
+    def push_if(cond, src, dst, sid, dev):
+        copy = (src, dst, sid, dev, SHARED + 1 + len(maybes))
+
         @pl.when(cond)
         def _():
-            remote(*args).start()
-
-        maybes.append((cond, args))
+            remote(*copy).start()
+
+        maybes.append((cond, copy))
 
     def arrive_if(cond, *args):
         @pl.when(cond)
@@ -98,9 +107,11 @@
 
     local_count = [0]
 
-    def local(src, dst):
-        copy = pltpu.make_async_copy(src, dst, local_sem.at[local_count[0]])
-        local_count[0] += 1
+    def local(src, dst, sem=None):
+        if sem is None:
+            sem = local_sem.at[local_count[0]]
+            local_count[0] += 1
+        copy = pltpu.make_async_copy(src, dst, sem)
         copy.start()
         return copy
 
@@ -167,24 +178,22 @@
         pl.semaphore_signal(barrier, inc=1, device_id=to_cross((y_lo + k) % 4), device_id_type=MESH)
     pl.semaphore_wait(barrier, 33)
 
-    kv_sid, q_sid = new(16), new(8)
+    k_sid, v_sid, q_sid = new(), new(), new()
     for k in range(1, 8):
         peer = (head + k) % 8
         cols = pl.ds(pl.multiple_of(peer * 128, 128), 128)
-        push(k_ref.at[:, cols], keys_all.at[0, y_lo, head], kv_sid + k, to_head(peer))
-        push(v_ref.at[:, cols], values_near.at[y, head], kv_sid + 8 + k, to_head(peer))
+        push(k_ref.at[:, cols], keys_all.at[0, y_lo, head], k_sid, to_head(peer))
+        push(v_ref.at[:, cols], values_near.at[y, head], v_sid, to_head(peer))
     own = pl.ds(pl.multiple_of(head * 128, 128), 128)
-    own_copies = [
-        local(k_ref.at[:, own], keys_all.at[0, y_lo, head]),
-        local(v_ref.at[:, own], values_near.at[y, head]),
-    ]
+    local(k_ref.at[:, own], keys_all.at[0, y_lo, head], recv_sem.at[k_sid])
+    local(v_ref.at[:, own], values_near.at[y, head], recv_sem.at[v_sid])
     for k in range(1, 8):
         peer = (head + k) % 8
         cols = pl.ds(pl.multiple_of(peer * 512, 512), 512)
-        push(q_ref.at[:, cols], q_all.at[head], q_sid + k, to_head(peer))
-    own_copies.append(local(q_ref.at[:, pl.ds(pl.multiple_of(head * 512, 512), 512)], q_all.at[head]))
-
-    w_sid = new(24)
+        push(q_ref.at[:, cols], q_all.at[head], q_sid, to_head(peer))
+    local(q_ref.at[:, pl.ds(pl.multiple_of(head * 512, 512), 512)], q_all.at[head], recv_sem.at[q_sid])
+
+    w_sid = new()
 
     def w_cols(part, s):
         return pl.ds(pl.multiple_of(s * 768 + part * 128, 128), 128)
@@ -202,27 +211,20 @@
                 for part in parts:
                     remote(
                         w_sources(peer)[part], w_all.at[feat(y), z, :, w_cols(part, c)],
-                        w_sid + 3 * k + part, to_y(peer),
+                        w_sid, to_y(peer), SHARED,
                     ).start()
 
-    def w_own(part):
-        return pltpu.make_async_copy(
-            w_sources(y)[part], w_all.at[feat(y), z, :, w_cols(part, c)], local_sem.at[8 + part]
-        )
-
-    def w_exchanged(parts):
+    def w_exchanged():
         @pl.when(y != NY - 1)
         def _():
-            for part in parts:
-                w_own(part).wait()
-                for k in range(1, NY):
-                    dst = w_all.at[feat((y + NY - k) % NY), z, :, w_cols(part, c)]
-                    arrive(dst, w_sid + 3 * k + part)
+            arrive(w_part(z, c, 0, 384), w_sid)
 
     @pl.when(y != NY - 1)
     def _():
-        for part in range(3):
-            w_own(part).start()
+        for part, src in enumerate(w_sources(y)):
+            pltpu.make_async_copy(
+                src, w_all.at[feat(y), z, :, w_cols(part, c)], recv_sem.at[w_sid]
+            ).start()
 
     @pl.when(y == NY - 1)
     def _():
@@ -237,35 +239,20 @@
     wo_copy = local(wo_ref, wo_all.at[y_hi, z, :, lanes(c, 512)])
     res_copy = local(resid_ref.at[pl.ds(pl.multiple_of(head * 64, 64), 64)], res)
 
-    for copy in own_copies:
-        copy.wait()
-    for k in range(1, 8):
-        peer = (head + 8 - k) % 8
-        arrive(keys_all.at[0, y_lo, peer], kv_sid + k)
-        arrive(values_near.at[y, peer], kv_sid + 8 + k)
-
-    def shared_ring(buf_chunk, then=None, buf_half=None):
-        sid = new(8)
-
+    arrive(keys_all.at[0, y_lo], k_sid)
+    arrive(values_near.at[y], v_sid)
+
+    def shared_ring(buf_chunk, sid, then=None, buf_half=None):
         def arrived(i, n):
-            push(buf_chunk(i, c), buf_chunk(i, c), sid + n, sibling)
+            push(buf_chunk(i, c), buf_chunk(i, c), sid, sibling)
             if then is not None:
                 then(i, n)
 
         half = None if buf_half is None else lambda i, b: buf_half(i, b, c)
-        gen = ring(NZ, z, to_z, lambda i: buf_chunk(i, c), half, arrived)
-
-        def wait_sibling():
-            for n in range(8):
-                step = (n + 1) // 2
-                i = (z + step) % NZ if n % 2 else (z - step + NZ) % NZ
-                arrive(buf_chunk(i, other), sid + n)
-
-        return gen, wait_sibling
-
-    wo_ring, wo_wait = shared_ring(
-        lambda i, s: wo_all.at[:, i, :, lanes(s, 512)]
-    )
+        return ring(NZ, z, to_z, lambda i: buf_chunk(i, c), half, arrived)
+
+    wo_core_sid = new()
+    wo_ring = shared_ring(lambda i, s: wo_all.at[:, i, :, lanes(s, 512)], wo_core_sid)
 
     ahead_sid, key_sid, near_sid, far_sid = new(BACK), new(4 * BACK), new(8), new(BACK + 1)
 
@@ -331,21 +318,21 @@
     def w_part(i, s, first, width, f=0, count=8):
         return w_all.at[pl.ds(f, count), i, :, pl.ds(pl.multiple_of(s * 768 + first, 128), width)]
 
-    over_sid, mirror_sid, w_core_sid = new(2), new(24), new(24)
+    over_sid, mirror_sid, w_core_sid = new(2), new(24), new()
     to_mirror = to_x(mirror)
     next(wo_ring)
     gain_sid = new(4)
     for k in range(1, 4):
         push(gain_ref, gains.at[y_lo], gain_sid + k, to_lo((y_lo + k) % 4))
     gains[y_lo] = gain_ref[...]
-    w_exchanged([0, 1, 2])
+    w_exchanged()
     push(w_part(z, c, 256, 128), w_part(z, c, 384, 128), over_sid, to_mirror)
     push(w_part(z, c, 0, 256, 6, 2), w_part(z, c, 512, 256, 6, 2), over_sid + 1, to_mirror)
 
     def w_quarter_ring(p):
         if p == 3:
             return shared_ring(
-                lambda i, s: w_part(i, s, 0, 768, 6, 2), None,
+                lambda i, s: w_part(i, s, 0, 768, 6, 2), w_core_sid, None,
                 lambda i, b, s: w_part(i, s, 0, 768, 6 + b, 1),
             )
 
@@ -356,7 +343,7 @@
             )
 
         return shared_ring(
-            lambda i, s: w_part(i, s, 0, 512, 2 * p, 2), w_arrived,
+            lambda i, s: w_part(i, s, 0, 512, 2 * p, 2), w_core_sid, w_arrived,
             lambda i, b, s: w_part(i, s, 0, 512, 2 * p + b, 1),
         )
 
@@ -367,11 +354,11 @@
         return (z + step) % NZ if n % 2 else (z - step + NZ) % NZ
 
     def w_step(p, *which):
-        next(w_rings[p][0], None)
+        next(w_rings[p], None)
         for n in which if p < 3 else ():
             gate_up_part = w_part(w_place(n), c, 512, 256, 2 * p, 2)
             arrive(gate_up_part, mirror_sid + 8 * p + n)
-            push(gate_up_part, gate_up_part, w_core_sid + 8 * p + n, sibling)
+            push(gate_up_part, gate_up_part, w_core_sid, sibling)
 
     arrive(w_part(z, c, 384, 128), over_sid)
     arrive(w_part(z, c, 512, 256, 6, 2), over_sid + 1)
@@ -384,8 +371,7 @@
             peer = (y_lo + 4 - k) % 4
             arrive_if(key_wanted(dz, peer, y_lo), keys_all.at[dz, peer], key_sid + 4 * dz + k)
 
-    for k in range(1, 8):
-        arrive(q_all.at[(head + 8 - k) % 8], q_sid + k)
+    arrive(q_all, q_sid)
     place = outer * 512 + y_lo * 128 + lax.broadcasted_iota(jnp.int32, (128, 1), 0)
     start = jnp.zeros((128, 1), jnp.int32)
     bound = jnp.int32(0)
@@ -408,10 +394,12 @@
         for dz in range(BACK):
             values = (values_near[pl.ds(y_hi * 4, 4)] if dz == 0 else values_far[dz - 1]).reshape(512, 128)
             summed += jnp.dot(e[:, dz * 512:(dz + 1) * 512], values, preferred_element_type=F32)
-        ctx_ref[:, g * 128:(g + 1) * 128] = (summed / total).astype(BF)
+        ctx_own[:, g * 128:(g + 1) * 128] = (summed / total).astype(BF)
 
     def half_rows(i):
-        return ctx_ref.at[pl.ds(pl.multiple_of(i * 64, 64), 64)]
+        return ctx_own.at[pl.ds(pl.multiple_of(i * 64, 64), 64)]
+
+    ctx_copy = local(ctx_own, ctx_ref)
 
     def ctx_part(i, core):
         return ctx_all.at[i, :, lanes(core, 512)]
@@ -431,10 +419,10 @@
 
     def proj_push(i):
         way = (i + NX - x) % NX
-        return remote(proj.at[i], proj_in.at[way], proj_sid + way, to_x(i))
+        return remote(proj.at[i], proj_in.at[way], proj_sid + way, to_x(i), PROJ)
 
     finish(wo_ring)
-    wo_wait()
+    arrive(wo_all.at[:, :, :, lanes(other, 512)], wo_core_sid)
     for k in range(4):
         i = (y_lo + 4 - k) % 4
         if k > 0:
@@ -461,11 +449,11 @@
         part = hid.at[i % 4, b, i // 4, p]
         return part if half is None else part.at[pl.ds(half * 32, 32)]
 
-    first_sid, second_sid = new(), new(8)
+    first_sid, second_sid = new(), new()
     to_pair = to_x(pair)
 
     def along_x(i, n):
-        push(hid_part(i, 1, u), hid_part(i, 1, u), second_sid + n, to_pair)
+        push(hid_part(i, 1, u), hid_part(i, 1, u), second_sid, to_pair)
 
     push(hid_part(y, 0, u), hid_part(y, 0, u), first_sid, to_pair)
     y_first = ring(
@@ -498,19 +486,14 @@
             w_step(1, 5, 6)
     for gen in x_first:
         next(gen, None)
-    for n in range(8):
-        step = (n + 1) // 2
-        i = (y + step) % NY if n % 2 else (y - step + NY) % NY
-        arrive(hid_part(i, 1, 1 - u), second_sid + n)
+    arrive(hid.at[:, 1, :, 1 - u], second_sid)
     for k in range(1, 4):
         arrive(gains.at[(y_lo + 4 - k) % 4], gain_sid + k)
     w_step(2, 5, 6)
     w_step(3, 5, 6)
     for p in range(4):
         w_step(p, 7)
-        w_rings[p][1]()
-        for n in range(8 if p < 3 else 0):
-            arrive(w_part(w_place(n), other, 512, 256, 2 * p, 2), w_core_sid + 8 * p + n)
+    arrive(w_all.at[:, :, :, lanes(other, 768)], w_core_sid)
 
     acc[...] = jnp.zeros_like(acc)
 
@@ -623,32 +606,43 @@
     total = odd_sum[u].astype(F32) + odd_in[...].astype(F32)
     out_ref[:, 512:] = (hid[y_lo, 1, y_hi, u].astype(F32) + total).astype(BF)
 
-    for copy in sends:
-        copy.wait_send()
-    for cond, args in maybes:
+    ctx_copy.wait()
+    if sent[-1] == 0:
+        sent.pop()
+    for ssid, units in enumerate(sent):
+        block = w_all.at[tuple(pl.ds(0, n) for n in block_shape(units))]
+        remote(block, block, 0, sibling, ssid).wait_send()
+    for cond, copy in maybes:
         @pl.when(cond)
-        def _(args=args):
-            remote(*args).wait_send()
-
-    for i in range(NX):
-        @pl.when(i != x)
-        def _(i=i):
-            proj_push(i).wait_send()
-
-    for k in range(1, NY):
-        peer = (y + k) % NY
-
-        @pl.when(peer != NY - 1)
-        def _(k=k, peer=peer):
-            for part, src in enumerate(w_sources(peer)):
-                remote(
-                    src, w_all.at[feat(y), z, :, w_cols(part, c)], w_sid + 3 * k + part, to_y(peer)
-                ).wait_send()
-
-    assert counter[0] <= SEMS, counter[0]
-
-
-SEMS = 460
+        def _(copy=copy):
+            remote(*copy).wait_send()
+
+    remote(proj.at[pl.ds(0, 3)], proj.at[pl.ds(0, 3)], 0, sibling, PROJ).wait_send()
+
+    for last, count in ((False, 6), (True, 7)):
+        @pl.when((y == NY - 1) == last)
+        def _(count=count):
+            pieces = w_all.at[pl.ds(0, count), 0, :, pl.ds(0, 384)]
+            remote(pieces, pieces, 0, sibling, SHARED).wait_send()
+
+    assert counter[0] == RECV and len(sent) == SHARED and local_count[0] == LOCAL, (counter[0], len(sent), sent)
+    assert PROJ + 1 == SEND and len(maybes) == MAYBES, len(maybes)
+
+
+RECV, LOCAL, MAYBES, SHARED, FULL = 183, 3, 28, 17, 253
+PROJ = SHARED + 1 + MAYBES
+SEND = PROJ + 1
+
+
+def block_shape(units):
+    shapes = (
+        (a, b, 16 * r, 128 * t)
+        for a in range(1, 9) for b in range(1, 9) for r in range(1, 5) for t in range(1, 13)
+        if a * b * r * t == units
+    )
+    return next(shapes, None)
+
+
 SLOTS = (0, 512, 768, 1280)
 
 
@@ -667,7 +661,7 @@
             jax.ShapeDtypeStruct((64, 1024), BF),
         ),
         in_specs=[anywhere, anywhere, anywhere, smem, anywhere, vmem, anywhere, anywhere, anywhere],
-        out_specs=(vmem, vmem),
+        out_specs=(anywhere, vmem),
         scratch_shapes=[
             buf(8, 16, 512),
             buf(BACK, 4, 8, 16, 128),
@@ -675,6 +669,7 @@
             buf(BACK - 1, 4, 8, 16, 128),
             buf(4, 8, 16, 128),
             buf(4, 128, BACK * 512, kind=F32),
+            buf(128, 512),
             buf(4, 64, 1024),
             buf(2, 8, 64, 1024),
             buf(8, 8, 64, 1536),
@@ -691,9 +686,9 @@
             buf(3, 2, 4, 64, 512),
             buf(2, 64, 512),
             buf(64, 512),
-            pltpu.SemaphoreType.DMA((SEMS,)),
-            pltpu.SemaphoreType.DMA((SEMS,)),
-            pltpu.SemaphoreType.DMA((16,)),
+            pltpu.SemaphoreType.DMA((SEND,)),
+            pltpu.SemaphoreType.DMA((RECV,)),
+            pltpu.SemaphoreType.DMA((LOCAL,)),
         ],
         compiler_params=pltpu.CompilerParams(
             collective_id=0, has_side_effects=True, vmem_limit_bytes=56 * 1024 * 1024

time: 150 us -> 143 us (0.953)
  Pallas kernels: 146 us -> 140 us
    pallas_call x1, Pallas kernels: 146 us -> 140 us  [per_device(): pl.pallas_call(kernel, out_shape=(jax.ShapeDtypeStruct((128, 512), BF), j...]
where the time goes in v4:
time: 143 us
  Pallas kernels  140 us (98%)
  local copies, waits for them, and re-layouts  2.26 us (2%)
    pallas_call x1, Pallas kernels, per_device(): pl.pallas_call(kernel, out_shape=(jax.ShapeDtypeStruct((128, 512), BF), j...  140 us

profile of v4, /device:TPU:1, one launch (start us, length us, event | category | flops | bytes accessed | tf_op | source)
XLA Modules:
  0.0 143.1 jit_solution(18358858911566054414)
XLA Ops:
  0.6 140.2 %shard_map.104 = (bf16[128,512]{1,0:T(8,128)(2,1)}, bf16[64,1024]{1,0:T(8,128)(2,1)}) custom-call(bf16[16,4096]{1,0:T(8,128)(2,1)} %q_ref.1, bf16[16,1024]{1,0:T(8,128)(2,1)} %k_ref.1, bf16[16,1024]{1,0:T(8,128)(2,1)} %v_ref.1, s32[24]{0:T(128)} %docs_ref.1, bf16[512,1024]{1,0:T(8,128)(2,1)} %resid_ref.1, f32[8,128]{1,0:T(8,128)} %bitcast.5, ...), custom_call_target="tpu_custom_call" | custom-call | flops 4000000000 | bytes 4000000 | tf_op jit(solution)/shard_map/pallas_call | solution.py:657
  140.8 0.0 copy-start
  140.8 1.6 %copy.13 = bf16[128,512]{1,0:T(8,128)(2,1)} copy(bf16[128,512]{1,0:T(8,128)(2,1)} %get-tuple-element.4) | data formatting | bytes 262144
  142.4 0.0 copy-done
  142.5 0.7 copy.14
Async XLA Ops:
  140.8 1.6 %copy-start = (bf16[64,1024]{1,0:T(8,128)(2,1)S(1)}, bf16[64,1024]{1,0:T(8,128)(2,1)}, u32[]{:S(2)}) copy-start(bf16[64,1024]{1,0:T(8,128)(2,1)} %get-tuple-element.5) | copy-start | bytes 393220

commit v5 on v4

--- a/solution.py
+++ b/solution.py
@@ -24,8 +24,8 @@
 def kernel(
     q_ref, k_ref, v_ref, docs_ref, resid_ref, gain_ref, wo_ref, wgu_ref, wd_ref,
     ctx_ref, out_ref,
-    q_all, keys_all, values_near, values_far, relay, scores, ctx_own, ctx_all, wo_all, w_all, res, gains,
-    proj, proj_in, hid, acc, act, down, x_in, x_sum, rings, odd_sum, odd_in,
+    q_all, keys_all, values_near, values_far, relay, scores, softs, ctx_own, ctx_all, wo_all, w_all, res, gains,
+    proj, proj_in, hid, scaled, acc, act, down, x_in, x_sum, rings, odd_sum, odd_in,
     send_sem, recv_sem, local_sem,
 ):
     head = lax.axis_index("head")
@@ -318,54 +318,53 @@
     def w_part(i, s, first, width, f=0, count=8):
         return w_all.at[pl.ds(f, count), i, :, pl.ds(pl.multiple_of(s * 768 + first, 128), width)]
 
-    over_sid, mirror_sid, w_core_sid = new(2), new(24), new()
+    over_sid, mirror_sid, w_core_sid = new(2), new(24), new(4)
     to_mirror = to_x(mirror)
+    w_exchanged()
+    push(w_part(z, c, 256, 128), w_part(z, c, 384, 128), over_sid, to_mirror)
+    push(w_part(z, c, 0, 256, 6, 2), w_part(z, c, 512, 256, 6, 2), over_sid + 1, to_mirror)
+
+    def w_quarter_ring(p):
+        if p == 3:
+            return shared_ring(
+                lambda i, s: w_part(i, s, 0, 768, 6, 2), w_core_sid + 3, None,
+                lambda i, b, s: w_part(i, s, 0, 768, 6 + b, 1),
+            )
+
+        def w_arrived(i, n):
+            push(
+                w_part(i, c, 0, 256, 2 * p, 2), w_part(i, c, 512, 256, 2 * p, 2),
+                mirror_sid + 8 * p + n, to_mirror,
+            )
+
+        return shared_ring(
+            lambda i, s: w_part(i, s, 0, 512, 2 * p, 2), w_core_sid + p, w_arrived,
+            lambda i, b, s: w_part(i, s, 0, 512, 2 * p + b, 1),
+        )
+
+    w_rings = [w_quarter_ring(p) for p in range(4)]
+
+    def w_place(n):
+        step = (n + 1) // 2
+        return (z + step) % NZ if n % 2 else (z - step + NZ) % NZ
+
+    def w_step(p, *which):
+        next(w_rings[p], None)
+        for n in which if p < 3 else ():
+            gate_up_part = w_part(w_place(n), c, 512, 256, 2 * p, 2)
+            arrive(gate_up_part, mirror_sid + 8 * p + n)
+            push(gate_up_part, gate_up_part, w_core_sid + p, sibling)
+
     next(wo_ring)
     gain_sid = new(4)
     for k in range(1, 4):
         push(gain_ref, gains.at[y_lo], gain_sid + k, to_lo((y_lo + k) % 4))
     gains[y_lo] = gain_ref[...]
-    w_exchanged()
-    push(w_part(z, c, 256, 128), w_part(z, c, 384, 128), over_sid, to_mirror)
-    push(w_part(z, c, 0, 256, 6, 2), w_part(z, c, 512, 256, 6, 2), over_sid + 1, to_mirror)
-
-    def w_quarter_ring(p):
-        if p == 3:
-            return shared_ring(
-                lambda i, s: w_part(i, s, 0, 768, 6, 2), w_core_sid, None,
-                lambda i, b, s: w_part(i, s, 0, 768, 6 + b, 1),
-            )
-
-        def w_arrived(i, n):
-            push(
-                w_part(i, c, 0, 256, 2 * p, 2), w_part(i, c, 512, 256, 2 * p, 2),
-                mirror_sid + 8 * p + n, to_mirror,
-            )
-
-        return shared_ring(
-            lambda i, s: w_part(i, s, 0, 512, 2 * p, 2), w_core_sid, w_arrived,
-            lambda i, b, s: w_part(i, s, 0, 512, 2 * p + b, 1),
-        )
-
-    w_rings = [w_quarter_ring(p) for p in range(4)]
-
-    def w_place(n):
-        step = (n + 1) // 2
-        return (z + step) % NZ if n % 2 else (z - step + NZ) % NZ
-
-    def w_step(p, *which):
-        next(w_rings[p], None)
-        for n in which if p < 3 else ():
-            gate_up_part = w_part(w_place(n), c, 512, 256, 2 * p, 2)
-            arrive(gate_up_part, mirror_sid + 8 * p + n)
-            push(gate_up_part, gate_up_part, w_core_sid, sibling)
-
     arrive(w_part(z, c, 384, 128), over_sid)
     arrive(w_part(z, c, 512, 256, 6, 2), over_sid + 1)
     for p in range(4):
         w_step(p)
-    for dz in (1, 3, 4):
-        arrive(values_far.at[dz - 1], far_sid + dz)
+
     for dz in range(BACK):
         for k in range(1, 4):
             peer = (y_lo + 4 - k) % 4
@@ -385,16 +384,21 @@
         for g in range(4):
             heads_q = q_all[:, :, g * 128:(g + 1) * 128].reshape(128, 128)
             scores[g, :, dz * 512:(dz + 1) * 512] = nt(heads_q, keys) * SCALE + bias
+    totals = []
     for g in range(4):
         s = scores[g]
         e = jnp.exp(s - jnp.max(s, axis=1, keepdims=True))
-        total = jnp.sum(e, axis=1, keepdims=True)
-        e = e.astype(BF)
+        totals.append(jnp.sum(e, axis=1, keepdims=True))
+        softs[g] = e.astype(BF)
+
+    for dz in (1, 3, 4):
+        arrive(values_far.at[dz - 1], far_sid + dz)
+    for g in range(4):
         summed = jnp.zeros((128, 128), F32)
         for dz in range(BACK):
             values = (values_near[pl.ds(y_hi * 4, 4)] if dz == 0 else values_far[dz - 1]).reshape(512, 128)
-            summed += jnp.dot(e[:, dz * 512:(dz + 1) * 512], values, preferred_element_type=F32)
-        ctx_own[:, g * 128:(g + 1) * 128] = (summed / total).astype(BF)
+            summed += jnp.dot(softs[g, :, dz * 512:(dz + 1) * 512], values, preferred_element_type=F32)
+        ctx_own[:, g * 128:(g + 1) * 128] = (summed / totals[g]).astype(BF)
 
     def half_rows(i):
         return ctx_own.at[pl.ds(pl.multiple_of(i * 64, 64), 64)]
@@ -482,25 +486,23 @@
             w_step(2 * s - 2, 3, 4)
             w_step(2 * s - 1, 3, 4)
         if s == 3:
-            w_step(0, 5, 6)
-            w_step(1, 5, 6)
+            w_step(0)
+            w_step(1)
     for gen in x_first:
         next(gen, None)
     arrive(hid.at[:, 1, :, 1 - u], second_sid)
     for k in range(1, 4):
         arrive(gains.at[(y_lo + 4 - k) % 4], gain_sid + k)
-    w_step(2, 5, 6)
-    w_step(3, 5, 6)
-    for p in range(4):
-        w_step(p, 7)
-    arrive(w_all.at[:, :, :, lanes(other, 768)], w_core_sid)
-
+    w_step(2)
+    w_step(3)
+    for p in range(3):
+        w_step(p, 5, 6)
     acc[...] = jnp.zeros_like(acc)
 
-    def gate_up(f, squares):
+    def scale(f, squares):
         gain_row = gains[f // 2]
         rows = hid[f // 2, f % 2].reshape(256, 512).astype(F32)
-        scaled = jnp.concatenate(
+        scaled[f] = jnp.concatenate(
             [
                 rows[:, j * 128:(j + 1) * 128]
                 * jnp.where(f % 2 == 0, gain_row[j:j + 1], gain_row[4 + j:5 + j])
@@ -508,12 +510,21 @@
             ],
             axis=1,
         ).astype(BF)
+        return squares + jnp.sum(rows * rows, axis=1, keepdims=True)
+
+    squares = lax.fori_loop(0, 8, scale, jnp.zeros((256, 1), F32))
+
+    def gate_up(f, _):
         for s, first in enumerate(SLOTS):
             weights = w_all[f, :, :, first:first + 256].reshape(512, 256)
-            acc[s] += jnp.dot(scaled, weights, preferred_element_type=F32)
-        return squares + jnp.sum(rows * rows, axis=1, keepdims=True)
-
-    squares = lax.fori_loop(0, 8, gate_up, jnp.zeros((256, 1), F32))
+            acc[s] += jnp.dot(scaled[f], weights, preferred_element_type=F32)
+        return 0
+
+    for p in (3, 0, 1, 2):
+        w_step(p, 7)
+        arrive(w_all.at[pl.ds(2 * p, 2), :, :, lanes(other, 768)], w_core_sid + p)
+    lax.fori_loop(0, 8, gate_up, 0)
+
     inverse = lax.rsqrt(squares / D + 1e-05)
     for s in range(4):
         gate, up = acc[s, :, :128] * inverse, acc[s, :, 128:] * inverse
@@ -629,7 +640,7 @@
     assert PROJ + 1 == SEND and len(maybes) == MAYBES, len(maybes)
 
 
-RECV, LOCAL, MAYBES, SHARED, FULL = 183, 3, 28, 17, 253
+RECV, LOCAL, MAYBES, SHARED, FULL = 186, 3, 28, 18, 244
 PROJ = SHARED + 1 + MAYBES
 SEND = PROJ + 1
 
@@ -669,6 +680,7 @@
             buf(BACK - 1, 4, 8, 16, 128),
             buf(4, 8, 16, 128),
             buf(4, 128, BACK * 512, kind=F32),
+            buf(4, 128, BACK * 512),
             buf(128, 512),
             buf(4, 64, 1024),
             buf(2, 8, 64, 1024),
@@ -678,6 +690,7 @@
             buf(4, 64, 1024),
             buf(4, 64, 1024),
             buf(4, 2, 2, 2, 64, 512),
+            buf(8, 256, 512),
             buf(4, 256, 256, kind=F32),
             buf(256, 512),
             buf(4, 2, 2, 2, 64, 512),

time: 143 us -> 142 us (level)
    pallas_call x1, Pallas kernels: 140 us -> 139 us  [per_device(): pl.pallas_call(kernel, out_shape=(jax.ShapeDtypeStruct((128, 512), BF), j...]
where the time goes in v5:
time: 142 us
  Pallas kernels  139 us (98%)
  local copies, waits for them, and re-layouts  2.26 us (2%)
    pallas_call x1, Pallas kernels, per_device(): pl.pallas_call(kernel, out_shape=(jax.ShapeDtypeStruct((128, 512), BF), j...  139 us

profile of v5, /device:TPU:1, one launch (start us, length us, event | category | flops | bytes accessed | tf_op | source)
XLA Modules:
  0.0 141.6 jit_solution(18152958478619655945)
XLA Ops:
  0.6 138.7 %shard_map.104 = (bf16[128,512]{1,0:T(8,128)(2,1)}, bf16[64,1024]{1,0:T(8,128)(2,1)}) custom-call(bf16[16,4096]{1,0:T(8,128)(2,1)} %q_ref.1, bf16[16,1024]{1,0:T(8,128)(2,1)} %k_ref.1, bf16[16,1024]{1,0:T(8,128)(2,1)} %v_ref.1, s32[24]{0:T(128)} %docs_ref.1, bf16[512,1024]{1,0:T(8,128)(2,1)} %resid_ref.1, f32[8,128]{1,0:T(8,128)} %bitcast.5, ...), custom_call_target="tpu_custom_call" | custom-call | flops 4000000000 | bytes 4000000 | tf_op jit(solution)/shard_map/pallas_call | solution.py:668
  139.3 0.0 copy-start
  139.3 1.6 %copy.13 = bf16[128,512]{1,0:T(8,128)(2,1)} copy(bf16[128,512]{1,0:T(8,128)(2,1)} %get-tuple-element.4) | data formatting | bytes 262144
  140.9 0.0 copy-done
  140.9 0.7 copy.14
Async XLA Ops:
  139.3 1.6 %copy-start = (bf16[64,1024]{1,0:T(8,128)(2,1)S(1)}, bf16[64,1024]{1,0:T(8,128)(2,1)}, u32[]{:S(2)}) copy-start(bf16[64,1024]{1,0:T(8,128)(2,1)} %get-tuple-element.5) | copy-start | bytes 393220
